TPU v7x, 32 devices: a whole 2x2x4 slice. The times are simulated.
32 devices in a mesh: ctx: 8 (over z, core), fsdp: 4 (over y, x).
Axes of the slice: x: 2, y: 2, z: 4, core: 2. Of those that a mesh axis runs over, the one named last changes fastest.
Arguments:
- tokens: bfloat16 [2048, 8, 1088], P('ctx', 'fsdp'), may hold values from -6 to 6
- cotangent: bfloat16 [2048, 8, 1088], P('ctx', 'fsdp'), may hold values from -6 to 6
- lengths: int32 [8], P('fsdp'), may hold values from 512 to 2048, as said below
- w_rows: float32 [1088, 8704], P('fsdp')
- rows_first: bfloat16 [1088, 8704], P('fsdp')
- rows_second: float32 [1088, 8704], P('fsdp'), may hold values from 204 to 819
- w_down: float32 [4352, 1088], P(None, 'fsdp'), may hold values from -0.09375 to 0.09375
- down_first: bfloat16 [4352, 1088], P(None, 'fsdp')
- down_second: float32 [4352, 1088], P(None, 'fsdp'), may hold values from 204 to 819
- vectors: float32 [12, 1088], P(None, 'fsdp')
- vec_first: bfloat16 [12, 1088], P(None, 'fsdp')
- vec_second: float32 [12, 1088], P(None, 'fsdp'), may hold values from 204 to 819
Outputs:
- output: bfloat16 [2048, 8, 1088], P('ctx', 'fsdp')
- grad_tokens: bfloat16 [2048, 8, 1088], P('ctx', 'fsdp')
- rows_moment: float32 [1088, 8704], P('fsdp')
- rows_square: float32 [1088, 8704], P('fsdp')
- rows_new: float32 [1088, 8704], P('fsdp')
- down_moment: float32 [4352, 1088], P(None, 'fsdp')
- down_square: float32 [4352, 1088], P(None, 'fsdp')
- down_new: float32 [4352, 1088], P(None, 'fsdp')
- vec_moment: float32 [12, 1088], P(None, 'fsdp')
- vec_square: float32 [12, 1088], P(None, 'fsdp')
- vec_new: float32 [12, 1088], P(None, 'fsdp')
Inputs may be any that keep to these rules, and one draw needn't show every extreme that they name: `lengths`: in each group of 2 consecutive slots one slot, chosen by the seed, holds a sequence of 2048 positions; the others hold at least a quarter of 2048.
All inputs are finite; a program needn't handle non-finite values.
Results may differ from a plain program's by a relative error of at most 0.0095.
Values may be sent and summed in bfloat16 or wider, within the bound.
A program may use at most 384 MiB of HBM per device.

v0:
```python
import functools
import math

import jax
import jax.numpy as jnp
from jax import lax
from jax.experimental import pallas as pl
from jax.experimental.pallas import tpu as pltpu
from jax.sharding import PartitionSpec as P

HEADS = 17
HEAD_DIM = 64
FF = 4352
STEP = 10

MASKED = -1e30
NORM_EPS = 1e-05
BETA_ONE = 0.9
BETA_TWO = 0.95
ADAM_EPS = 1e-08
BF16 = jnp.bfloat16
F32 = jnp.float32


def dot(left, right, dims=((1,), (0,))):
    return lax.dot_general(left, right, (dims, ((), ())), preferred_element_type=F32)


def padded(top, rows, width):
    row = lax.broadcasted_iota(jnp.int32, (rows, width), 0)
    out = jnp.zeros((rows, width), F32)
    for index, value in enumerate(top):
        out = jnp.where(row == index, value, out)
    return out.astype(BF16)


def key_rows(lens_ref, key, length):
    pos = lax.broadcasted_iota(jnp.int32, (1, length), 1)
    bias = jnp.where(pos < lens_ref[0], 0.0, MASKED)
    one = jnp.ones((1, length), F32)
    extra = padded([bias, one, one, one], HEAD_DIM, length)
    return jnp.concatenate([key, extra], axis=0).T


def causal(block):
    key = lax.broadcasted_iota(jnp.int32, (block, block), 0)
    query = lax.broadcasted_iota(jnp.int32, (block, block), 1)
    return key <= query


def attend_kernel(block, lens_ref, q_ref, k_ref, v_ref, o_ref, low_ref, lse_ref, keys):
    heads, _, length = k_ref.shape[2:]
    tok = low_ref.shape[-1]
    step = pl.program_id(0)

    @pl.when(step == 0)
    def _():
        for h in range(heads):
            keys[h] = key_rows(lens_ref, k_ref[0, 0, h], length)

    one_row = padded([jnp.ones((1, block), F32)], HEAD_DIM, block)
    queries = []
    for h in range(heads):
        query = (q_ref[0, 0, h].astype(F32) * (1.0 / math.sqrt(HEAD_DIM))).astype(BF16)
        queries.append(jnp.concatenate([query, one_row], axis=0))

    def one(index, states, mask):
        start = pl.multiple_of(index * block, block)
        all_scores = [dot(keys[h, pl.ds(start, block), :], queries[h]) for h in range(heads)]
        results = []
        for h, (top, total, accum) in enumerate(states):
            scores = all_scores[h]
            if mask is not None:
                scores = jnp.where(mask, scores, MASKED)
            new_top = jnp.maximum(top, jnp.max(scores, axis=0, keepdims=True))
            weights = jnp.exp(scores - new_top)
            factor = jnp.exp(top - new_top)
            total = total * factor + jnp.sum(weights, axis=0, keepdims=True)
            value = v_ref[0, 0, h, :, pl.ds(start, block)]
            accum = accum * factor + dot(value, weights.astype(BF16))
            results.append((new_top, total, accum))
        return tuple(results)

    state = (
        jnp.full((1, block), MASKED, F32),
        jnp.zeros((1, block), F32),
        jnp.zeros((HEAD_DIM, block), F32),
    )
    states = lax.fori_loop(0, step, lambda i, s: one(i, s, None), (state,) * heads)
    states = one(step, states, causal(block))
    for h, (top, total, accum) in enumerate(states):
        result = accum / total
        o_ref[h] = result
        for i in range(block // tok):
            low_ref[i, h] = result[:, i * tok : (i + 1) * tok].astype(BF16)
        lse_ref[h] = top + jnp.log(total)


def head_specs(slot, heads, dim, length, block):
    def whole(part):
        return pl.BlockSpec((1, 1, heads, dim, length), lambda i, lens: (slot, part, 0, 0, 0))

    def piece(part):
        return pl.BlockSpec((1, 1, heads, dim, block), lambda i, lens: (slot, part, 0, 0, i))

    return whole, piece


def attend(lens, qkv, slot, tok):
    dim, length = qkv.shape[3:]
    pairs = lens.shape[0]
    block = math.gcd(length, 512)
    whole, piece = head_specs(slot, pairs, dim, length, block)
    return pl.pallas_call(
        functools.partial(attend_kernel, block),
        grid_spec=pltpu.PrefetchScalarGridSpec(
            num_scalar_prefetch=1,
            grid=(length // block,),
            in_specs=[piece(0), whole(1), whole(2)],
            out_specs=[
                pl.BlockSpec((pairs, dim, block), lambda i, lens: (0, 0, i)),
                pl.BlockSpec((block // tok, pairs, dim, tok), lambda i, lens: (i, 0, 0, 0)),
                pl.BlockSpec((pairs, 1, block), lambda i, lens: (0, 0, i)),
            ],
            scratch_shapes=[pltpu.VMEM((pairs, length, 2 * dim), BF16)],
        ),
        out_shape=[
            jax.ShapeDtypeStruct((pairs, dim, length), F32),
            jax.ShapeDtypeStruct((length // tok, pairs, dim, tok), BF16),
            jax.ShapeDtypeStruct((pairs, 1, length), F32),
        ],
        compiler_params=pltpu.CompilerParams(
            vmem_limit_bytes=48 * 2**20
        ),
        cost_estimate=pl.CostEstimate(flops=1000, bytes_accessed=1000, transcendentals=0),
    )(lens, qkv, qkv, qkv)


def split_three(value):
    first = value.astype(BF16).astype(F32)
    second = (value - first).astype(BF16).astype(F32)
    third = (value - first - second).astype(BF16).astype(F32)
    return [-first, -second, -third]


def attend_back_kernel(
    block,
    lens_ref,
    q_ref,
    k_ref,
    v_ref,
    o_ref,
    lse_ref,
    grad_ref,
    out_ref,
    keys,
    values,
    queries,
    grads,
    total,
):
    heads, dim, length = k_ref.shape[2:]
    tok = grad_ref.shape[-1]
    count = length // block
    step = pl.program_id(0)
    scale = 1.0 / math.sqrt(HEAD_DIM)

    @pl.when(step == 0)
    def _():
        one = jnp.ones((1, length), F32)
        for h in range(heads):
            keys[h] = key_rows(lens_ref, k_ref[0, 0, h], length)
            extra = padded([one, one, one], dim, length)
            values[h] = jnp.concatenate([v_ref[0, 0, h], extra], axis=0).T
            queries[h, 0:dim, :] = (q_ref[0, 0, h].astype(F32) * scale).astype(BF16)
            queries[h, dim:, :] = padded([one] + split_three(lse_ref[h]), dim, length)
            for i in range(length // tok):
                grads[h, 0:dim, i * tok : (i + 1) * tok] = grad_ref[i, h]
            delta = jnp.sum(grads[h, 0:dim, :].astype(F32) * o_ref[h], axis=0, keepdims=True)
            grads[h, dim:, :] = padded(split_three(delta), dim, length)
        total[...] = jnp.zeros_like(total)

    mine = pl.ds(pl.multiple_of(step * block, block), block)

    def one(index, states, mask):
        cols = pl.ds(pl.multiple_of(index * block, block), block)
        all_scores = [dot(keys[h, mine, :], queries[h, :, cols]) for h in range(heads)]
        results = []
        for h, (dk, dv) in enumerate(states):
            scores = all_scores[h]
            if mask is not None:
                scores = jnp.where(mask, scores, MASKED)
            probs = jnp.exp(scores)
            grad_scores = (probs * dot(values[h, mine, :], grads[h, :, cols])).astype(BF16)
            probs = probs.astype(BF16)
            dv = dv + dot(grads[h, 0:dim, cols], probs, ((1,), (1,)))
            dk = dk + dot(queries[h, 0:dim, cols], grad_scores, ((1,), (1,)))
            total[h, :, cols] += dot(k_ref[0, 0, h, :, mine], grad_scores)
            results.append((dk, dv))
        return tuple(results)

    zero = jnp.zeros((dim, block), F32)
    states = one(step, ((zero, zero),) * heads, causal(block))
    states = lax.fori_loop(step + 1, count, lambda i, s: one(i, s, None), states)
    for h, (dk, dv) in enumerate(states):
        dq = total[h, :, mine] * scale
        for i in range(block // tok):
            cols = slice(i * tok, (i + 1) * tok)
            out_ref[i, h, 0:dim] = dq[:, cols].astype(BF16)
            out_ref[i, h, dim : 2 * dim] = dk[:, cols].astype(BF16)
            out_ref[i, h, 2 * dim :] = dv[:, cols].astype(BF16)


def attend_back(lens, qkv, slot, out, lse, grad):
    dim, length = qkv.shape[3:]
    pairs, tok = lens.shape[0], grad.shape[-1]
    ctx = length // tok
    block = math.gcd(length, 512)
    whole, _ = head_specs(slot, pairs, dim, length, block)
    return pl.pallas_call(
        functools.partial(attend_back_kernel, block),
        grid_spec=pltpu.PrefetchScalarGridSpec(
            num_scalar_prefetch=1,
            grid=(length // block,),
            in_specs=[
                whole(0),
                whole(1),
                whole(2),
                pl.BlockSpec((pairs, dim, length), lambda i, lens: (0, 0, 0)),
                pl.BlockSpec((pairs, 1, length), lambda i, lens: (0, 0, 0)),
                pl.BlockSpec((ctx, pairs, dim, tok), lambda i, lens: (0, 0, 0, 0)),
            ],
            out_specs=pl.BlockSpec(
                (block // tok, pairs, 3 * dim, tok), lambda i, lens: (i, 0, 0, 0)
            ),
            scratch_shapes=[
                pltpu.VMEM((pairs, length, 2 * dim), BF16),
                pltpu.VMEM((pairs, length, 2 * dim), BF16),
                pltpu.VMEM((pairs, 2 * dim, length), BF16),
                pltpu.VMEM((pairs, 2 * dim, length), BF16),
                pltpu.VMEM((pairs, dim, length), F32),
            ],
        ),
        out_shape=jax.ShapeDtypeStruct((ctx, pairs, 3 * dim, tok), BF16),
        compiler_params=pltpu.CompilerParams(
            vmem_limit_bytes=48 * 2**20
        ),
        cost_estimate=pl.CostEstimate(flops=1000, bytes_accessed=1000, transcendentals=0),
    )(lens, qkv, qkv, qkv, out, lse, grad)


def own_grad_kernel(late_ref, first_ref, second_ref, first_grad_ref, second_grad_ref, last_grad_ref, out_ref, total):
    step = pl.program_id(0)
    nt = ((1,), (1,))
    first, second = first_ref[0, 0], second_ref[0, 0]
    head = dot(first, first_grad_ref[0], nt) + dot(second, second_grad_ref[0], nt)
    last = dot(jnp.where(late_ref[0] == 0, first, second), last_grad_ref[0], nt)
    part = jnp.concatenate([head, last], axis=1)

    @pl.when(step == 0)
    def _():
        total[...] = part

    @pl.when(step > 0)
    def _():
        total[...] += part

    @pl.when(step == pl.num_programs(0) - 1)
    def _():
        out_ref[...] = total[...]


def own_grad(late, act, first_grad, second_grad, last_grad):
    _, ctx, width, tok = act.shape
    feat, last = first_grad.shape[1], last_grad.shape[1]

    def block(rows):
        return pl.BlockSpec((1, rows, tok), lambda i, late: (i, 0, 0))

    def of(slot):
        return pl.BlockSpec((1, 1, width, tok), lambda i, late: (slot, i, 0, 0))

    return pl.pallas_call(
        own_grad_kernel,
        grid_spec=pltpu.PrefetchScalarGridSpec(
            num_scalar_prefetch=1,
            grid=(ctx,),
            in_specs=[of(0), of(1), block(feat), block(feat), block(last)],
            out_specs=pl.BlockSpec((width, feat + last), lambda i, late: (0, 0)),
            scratch_shapes=[pltpu.VMEM((width, feat + last), F32)],
        ),
        out_shape=jax.ShapeDtypeStruct((width, feat + last), F32),
        compiler_params=pltpu.CompilerParams(vmem_limit_bytes=48 * 2**20),
        cost_estimate=pl.CostEstimate(flops=1000, bytes_accessed=1000, transcendentals=0),
    )(late[None], act, act, first_grad, second_grad, last_grad)


def mlp_kernel(
    width,
    a_ref,
    g_ref,
    up_ref,
    down_ref,
    bias_ref,
    y_ref,
    ga_ref,
    dup_ref,
    ddown_ref,
    db_ref,
    a_rows,
    g_rows,
):
    step = pl.program_id(0)
    slots, _, tok = a_ref.shape
    block = up_ref.shape[1]

    @pl.when(step == 0)
    def _():
        for s in range(slots):
            a_rows[s * tok : (s + 1) * tok, :] = a_ref[s].T
            g_rows[s * tok : (s + 1) * tok, :] = g_ref[s].T
        y_ref[...] = jnp.zeros_like(y_ref)
        ga_ref[...] = jnp.zeros_like(ga_ref)

    def run(size):
        up = up_ref[:, :size]
        down = down_ref[:, :size]
        pre = dot(a_rows[...], up) + bias_ref[:, :size]
        cdf = 0.5 * (1.0 + lax.erf(pre * math.sqrt(0.5)))
        hidden = (pre * cdf).astype(BF16)
        slope = cdf + pre * jnp.exp(-0.5 * pre * pre) * (1.0 / math.sqrt(2.0 * math.pi))
        grad = (dot(g_rows[...], down) * slope).astype(BF16)
        db_ref[:, :size] = jnp.sum(grad.astype(F32), axis=0, keepdims=True)
        nt = ((1,), (1,))
        for s in range(slots):
            rows = slice(s * tok, (s + 1) * tok)
            y_ref[s] += dot(down, hidden[rows], nt)
            ga_ref[s] += dot(up, grad[rows], nt)
        dup = sum(dot(a_ref[s], grad[s * tok : (s + 1) * tok]) for s in range(slots))
        dup_ref[:, :size] = dup.astype(dup_ref.dtype)
        ddown = sum(dot(g_ref[s], hidden[s * tok : (s + 1) * tok]) for s in range(slots))
        ddown_ref[:, :size] = ddown.astype(ddown_ref.dtype)

    full = width // block

    @pl.when(step < full)
    def _():
        run(block)

    if width % block:

        @pl.when(step == full)
        def _():
            run(width % block)


def mlp(act, grad, up, down, bias):
    slots, width, tok = act.shape
    units = up.shape[1]
    block = 256

    def fixed(shape):
        return pl.BlockSpec(shape, lambda i: (0,) * len(shape))

    cols = pl.BlockSpec((width, block), lambda i: (0, i))
    line = pl.BlockSpec((1, block), lambda i: (0, i))
    total = jax.ShapeDtypeStruct((slots, width, tok), F32)
    grads = jax.ShapeDtypeStruct((width, units), BF16)
    return pl.pallas_call(
        functools.partial(mlp_kernel, units),
        grid=(pl.cdiv(units, block),),
        in_specs=[fixed(act.shape), fixed(act.shape), cols, cols, line],
        out_specs=[fixed(act.shape), fixed(act.shape), cols, cols, line],
        out_shape=[total, total, grads, grads, jax.ShapeDtypeStruct((1, units), F32)],
        scratch_shapes=[pltpu.VMEM((slots * tok, width), BF16)] * 2,
        compiler_params=pltpu.CompilerParams(vmem_limit_bytes=56 * 2**20),
        cost_estimate=pl.CostEstimate(flops=1000, bytes_accessed=1000, transcendentals=0),
    )(act, grad, up, down, bias)


def other_index(index, bit):
    return index + bit * (1 - 2 * lax.rem(index // bit, 2))


def split_columns(start, size, count):
    tiles = size // 128
    cuts = [start + 128 * (-(-tiles * i // count)) for i in range(count)] + [start + size]
    return [(cuts[i], cuts[i + 1] - cuts[i]) for i in range(count)]


def gather_kernel(
    ctx,
    fsdp,
    regular,
    x_ref,
    w_ref,
    v_ref,
    act_ref,
    qkv_ref,
    wo_ref,
    um_ref,
    uo_ref,
    vo_ref,
    xo_ref,
    wide,
    w_low,
    windows,
    own_w,
    own_t,
    v_all,
    v_rows,
    bias,
    acts,
    qkvs,
    x_send,
    x_recv,
    xc_send,
    xc_recv,
    w_send,
    w_recv,
    wc_send,
    wc_recv,
    v_send,
    v_recv,
    act_sem,
    local,
):
    c, f = lax.axis_index("ctx"), lax.axis_index("fsdp")
    chips = ctx // 2
    z, core = c // 2, lax.rem(c, 2)
    partner = 2 * z + 1 - core
    slots, width, tok = x_ref.shape
    rows = w_ref.shape[0]
    dim = HEAD_DIM
    owned = regular + 1
    levels = bits_of(fsdp)
    half = um_ref.shape[2]

    def combine(number):
        place = f
        for bit in range(levels):
            if number & (1 << bit):
                place = other_index(place, 1 << bit)
        return place

    barrier = pltpu.get_barrier_semaphore()

    def greet(where):
        pl.semaphore_signal(barrier, inc=1, device_id=where, device_id_type=pl.DeviceIdType.MESH)

    greet((partner, f))
    for number in range(1, fsdp):
        greet((c, combine(number)))

    @pl.when(z > 0)
    def _():
        greet((c - 2, f))

    @pl.when(z < chips - 1)
    def _():
        greet((c + 2, f))

    beside = (z > 0).astype(jnp.int32) + (z < chips - 1).astype(jnp.int32)
    pl.semaphore_wait(barrier, fsdp + beside)

    def remote(source, target, send, recv, where):
        return pltpu.make_async_remote_copy(
            src_ref=source,
            dst_ref=target,
            send_sem=send,
            recv_sem=recv,
            device_id=where,
            device_id_type=pl.DeviceIdType.MESH,
        )

    def x_copy(side, s, h):
        sign = 1 - 2 * side
        block = c - 2 * sign * s
        source = x_ref.at[h] if s == 0 else xo_ref.at[block, h]
        return remote(
            source, xo_ref.at[block, h], x_send.at[side, s, h], x_recv.at[side, s, h], (c + 2 * sign, f)
        )

    def x_sends(side, s):
        return (z - s >= 0) & (z < chips - 1) if side == 0 else (z + s < chips) & (z > 0)

    def x_gets(side, s):
        return z - 1 - s >= 0 if side == 0 else z + 1 + s < chips

    def x_arrival(side, s, h):
        sign = 1 - 2 * side
        block = c - 2 * sign * (s + 1)
        return remote(
            xo_ref.at[block, h],
            xo_ref.at[block, h],
            x_send.at[side, s, h],
            x_recv.at[side, s, h],
            (c + 2 * sign, f),
        )

    def x_share(side, s, h):
        sign = 1 - 2 * side
        block = c - 2 * sign * (s + 1)
        return remote(
            xo_ref.at[block, h],
            xo_ref.at[block, h],
            xc_send.at[side, s, h],
            xc_recv.at[side, s, h],
            (partner, f),
        )

    def x_share_arrival(side, s, h):
        sign = 1 - 2 * side
        block = partner - 2 * sign * (s + 1)
        return remote(
            xo_ref.at[block, h],
            xo_ref.at[block, h],
            xc_send.at[side, s, h],
            xc_recv.at[side, s, h],
            (partner, f),
        )

    def x_own(h):
        return remote(
            x_ref.at[h],
            xo_ref.at[c, h],
            xc_send.at[0, chips - 1, h],
            xc_recv.at[0, chips - 1, h],
            (partner, f),
        )

    def x_own_arrival(h):
        return remote(
            x_ref.at[h],
            xo_ref.at[partner, h],
            xc_send.at[0, chips - 1, h],
            xc_recv.at[0, chips - 1, h],
            (partner, f),
        )

    runs = split_columns(0, half, levels)

    def source(unit, stream):
        start, size = runs[stream]
        return w_low.at[:, pl.ds(pl.multiple_of((2 * unit + core) * half + start, 128), size)]

    def kept(unit, stream, place, which):
        start, size = runs[stream]
        if unit == 0:
            return wo_ref.at[place, :, pl.ds(pl.multiple_of(which * half + start, 128), size)]
        return um_ref.at[place, :, pl.ds(start, size)]

    def shared(unit, stream, place, which):
        start, size = runs[stream]
        if unit == 0:
            return kept(unit, stream, place, which)
        return uo_ref.at[place, :, pl.ds(start, size)]

    def w_copy(unit, stream, step, number):
        bit = 1 << ((stream + step) % levels)
        place = combine(number)
        there = kept(unit, stream, place, core)
        return remote(
            source(unit, stream) if number == 0 else there,
            there,
            w_send.at[unit, stream, number | bit],
            w_recv.at[unit, stream, number | bit],
            (c, other_index(f, bit)),
        )

    def w_arrival(unit, stream, number):
        block = kept(unit, stream, combine(number), core)
        sems = w_send.at[unit, stream, number], w_recv.at[unit, stream, number]
        return remote(block, block, *sems, (partner, f))

    def w_share(unit, stream, number):
        place = combine(number)
        sems = wc_send.at[unit, stream, number], wc_recv.at[unit, stream, number]
        block = kept(unit, stream, place, core)
        return remote(block, shared(unit, stream, place, core), *sems, (partner, f))

    def w_share_arrival(unit, stream, number):
        block = shared(unit, stream, combine(number), 1 - core)
        sems = wc_send.at[unit, stream, number], wc_recv.at[unit, stream, number]
        return remote(block, block, *sems, (partner, f))

    def held(stream, step):
        numbers = [0]
        for i in range(step):
            bit = 1 << ((stream + i) % levels)
            numbers += [n | bit for n in numbers]
        return numbers

    def v_copy(number):
        return remote(
            v_ref, v_all.at[f], v_send.at[number], v_recv.at[number], (c, combine(number))
        )

    def v_arrival(number):
        return remote(
            v_ref,
            v_all.at[combine(number)],
            v_send.at[number],
            v_recv.at[number],
            (c, combine(number)),
        )

    def x_begin(h):
        for side in range(2):

            @pl.when(x_sends(side, 0))
            def _(side=side):
                x_copy(side, 0, h).start()

        x_own(h).start()

    def x_step(h, s):
        for side in range(2):

            @pl.when(x_gets(side, s))
            def _(side=side):
                x_arrival(side, s, h).wait_recv()
                x_share(side, s, h).start()

            if s + 1 < chips - 1:

                @pl.when(x_sends(side, s + 1))
                def _(side=side):
                    x_copy(side, s + 1, h).start()

    def w_step(unit, step):
        for stream in range(levels):
            bit = 1 << ((stream + step) % levels)
            arrived = [number | bit for number in held(stream, step)]
            for number in arrived:
                w_arrival(unit, stream, number).wait_recv()
            if step + 1 < levels:
                for number in held(stream, step + 1):
                    w_copy(unit, stream, step + 1, number).start()
            for number in arrived:
                w_share(unit, stream, number).start()

    def fetch(unit):
        cols = pl.ds(2 * unit * half, 2 * half)
        return pltpu.make_async_copy(w_ref.at[:, cols], wide.at[:, cols], local.at[3 + unit])

    def w_begin(unit):
        fetch(unit).wait()
        cols = slice(2 * unit * half, 2 * (unit + 1) * half)

        strip = 16 if rows % 16 == 0 else rows

        def body(i, carry):
            at = pl.ds(pl.multiple_of(i * strip, strip), strip)
            w_low[at, cols] = wide[at, cols].astype(BF16)
            return carry

        lax.fori_loop(0, rows // strip, body, 0)
        for stream in range(levels):
            w_copy(unit, stream, 0, 0).start()

    own_up = w_low.at[:, pl.ds(pl.multiple_of((2 + core) * half, 128), half)]
    other_up = w_low.at[:, pl.ds(pl.multiple_of((3 - core) * half, 128), half)]
    kept_here = [
        pltpu.make_async_copy(w_low.at[:, pl.ds(0, 2 * half)], wo_ref.at[f], local.at[0]),
        pltpu.make_async_copy(own_up, um_ref.at[f], local.at[1]),
        pltpu.make_async_copy(other_up, uo_ref.at[f], local.at[2]),
    ]
    v_own = pltpu.make_async_copy(v_ref, v_all.at[f], local.at[5])
    v_out = pltpu.make_async_copy(v_all, vo_ref, local.at[6])
    x_here = pltpu.make_async_copy(x_ref, xo_ref.at[c], local.at[7])

    head_of = [i * ctx + c for i in range(regular)] + [HEADS - 1]
    places = [part * HEADS + head for part in range(3) for head in head_of]

    def window(i):
        start = pl.multiple_of(places[i] // 2 * 128, 128)
        return pltpu.make_async_copy(
            wo_ref.at[:, :, pl.ds(start, 128)], windows.at[i], local.at[8 + i]
        )

    def ready():
        kept_here[0].wait()
        for number in range(1, fsdp):
            v_arrival(number).wait_recv()
            for stream in range(levels):
                w_share_arrival(0, stream, number).wait_recv()
        v_own.wait()
        v_out.start()
        for i in range(len(places)):
            window(i).start()
        for i in range(fsdp):
            v_rows[i * rows : (i + 1) * rows, :] = v_all[i].astype(F32)
        own_w[...] = jnp.zeros_like(own_w)
        for i, place in enumerate(places):
            window(i).wait()
            odd = lax.rem(place, 2)
            for k in range(fsdp):
                both = windows[i, k]
                mine = jnp.where(odd == 0, both[:, :dim], both[:, dim:])
                own_w[k * rows : (k + 1) * rows, i * dim : (i + 1) * dim] = mine
        own_t[...] = own_w[...].T
        for part, column in ((0, 2), (2, 3)):
            for i, head in enumerate(head_of):
                start = (part * owned + i) * dim
                at = pl.ds(pl.multiple_of(head * dim, dim), dim)
                bias[start : start + dim, :] = v_rows[at, column : column + 1]
        start = owned * dim
        bias[start : 2 * start, :] = jnp.zeros((start, 1), F32)

    def project(h, b):
        unit, _ = norm_parts(xo_ref[b, h].astype(F32), 0)
        act = (unit * v_rows[:, 0:1] + v_rows[:, 1:2]).astype(BF16)
        acts[h, b] = act
        pltpu.make_async_copy(acts.at[h, b], act_ref.at[h, b], act_sem.at[h, b]).start()
        value = dot(own_t[...], act)[: 3 * owned * dim] + bias[...]
        qkvs[h, :, pl.ds(pl.multiple_of(b * tok, tok), tok)] = value.astype(BF16)

    def project_own(h):
        x_own_arrival(h).wait_recv()

        def body(i, carry):
            project(h, 2 * z + i)
            return carry

        lax.fori_loop(0, 2, body, 0)

    def project_step(h, s):
        for side in range(2):

            @pl.when(x_gets(side, s))
            def _(side=side):
                x_share_arrival(side, s, h).wait_recv()

        def body(i, carry):
            side = i // 2
            chip = z - (1 - 2 * side) * (s + 1)

            @pl.when((chip >= 0) & (chip < chips))
            def _():
                project(h, 2 * chip + lax.rem(i, 2))

            return carry

        lax.fori_loop(0, 4, body, 0)

    def out_copy(h):
        return pltpu.make_async_copy(qkvs.at[h], qkv_ref.at[h], local.at[8 + len(places) + h])

    plan = []
    block_time = 0.95

    def at(time, work, *values):
        plan.append((time, functools.partial(work, *values)))

    for h in range(slots):
        for s in range(chips - 1):
            at(block_time * (h * (chips - 1) + s + 1), x_step, h, s)
        if h > 0:
            at(block_time * (h * (chips - 1) - 1) + 0.01, x_begin, h)
    time = 0.0
    for unit in range(2):
        for step in range(levels):
            if unit == 0 and step == levels - 1:
                at(time + 0.9, w_begin, 1)
            time += 2.0 ** (step + 1) / levels
            at(time, w_step, unit, step)
        if unit == 0:
            done = max(time, block_time * (chips - 1))
    at(done + 0.3, ready)
    for h in range(slots):
        for s in range(-1, chips - 1):
            arrived = block_time * (h * (chips - 1) + s + 1) + 0.1
            late = max(arrived, done + 0.31 + 0.2 * (s + 1) + 0.01 * h)
            if s < 0:
                at(late, project_own, h)
            else:
                at(late, project_step, h, s)
        at(max(arrived, done + 0.31 + 0.2 * chips) + 0.02, lambda h: out_copy(h).start(), h)

    fetch(0).start()
    fetch(1).start()
    x_here.start()
    x_begin(0)
    for number in range(1, fsdp):
        v_copy(number).start()
    v_own.start()
    w_begin(0)
    kept_here[0].start()
    x_here.wait()
    for _, work in sorted(plan, key=lambda entry: entry[0]):
        work()

    kept_here[1].start()
    kept_here[2].start()
    kept_here[1].wait()
    kept_here[2].wait()
    v_out.wait()
    for number in range(1, fsdp):
        v_copy(number).wait_send()
        for unit in range(2):
            for stream in range(levels):
                w_arrival(unit, stream, number).wait_send()
                w_share(unit, stream, number).wait_send()
                if unit > 0:
                    w_share_arrival(unit, stream, number).wait_recv()
    for h in range(slots):
        x_own(h).wait_send()
        out_copy(h).wait()
        for b in range(ctx):
            pltpu.make_async_copy(acts.at[h, b], act_ref.at[h, b], act_sem.at[h, b]).wait()
        for s in range(chips - 1):
            for side in range(2):

                @pl.when(x_sends(side, s))
                def _(side=side, h=h, s=s):
                    x_copy(side, s, h).wait_send()

                @pl.when(x_gets(side, s))
                def _(side=side, h=h, s=s):
                    x_share(side, s, h).wait_send()


def gather_first(ctx, fsdp, regular, x, w, v):
    slots, width, tok = x.shape
    rows, columns = w.shape
    levels, chips = bits_of(fsdp), ctx // 2
    owned = regular + 1
    feat = 3 * owned * HEAD_DIM
    room = feat + -feat % 128
    anywhere = pl.BlockSpec(memory_space=pl.ANY)
    dma = pltpu.SemaphoreType.DMA
    return pl.pallas_call(
        functools.partial(gather_kernel, ctx, fsdp, regular),
        in_specs=[anywhere, anywhere, pl.BlockSpec(memory_space=pltpu.VMEM)],
        out_specs=[anywhere] * 6,
        out_shape=[
            jax.ShapeDtypeStruct((slots, ctx, width, tok), BF16),
            jax.ShapeDtypeStruct((slots, feat, ctx * tok), BF16),
            jax.ShapeDtypeStruct((fsdp, rows, columns // 2), BF16),
            jax.ShapeDtypeStruct((fsdp, rows, columns // 4), BF16),
            jax.ShapeDtypeStruct((fsdp, rows, columns // 4), BF16),
            jax.ShapeDtypeStruct((fsdp, rows, 128), BF16),
        ],
        scratch_shapes=[
            pltpu.VMEM((ctx, slots, width, tok), BF16),
            pltpu.VMEM((rows, columns), F32),
            pltpu.VMEM((rows, columns), BF16),
            pltpu.VMEM((3 * owned, fsdp, rows, 128), BF16),
            pltpu.VMEM((width, room), BF16),
            pltpu.VMEM((room, width), BF16),
            pltpu.VMEM((fsdp, rows, 128), BF16),
            pltpu.VMEM((width, 128), F32),
            pltpu.VMEM((feat, 1), F32),
            pltpu.VMEM((slots, ctx, width, tok), BF16),
            pltpu.VMEM((slots, feat, ctx * tok), BF16),
            dma((2, chips - 1, slots)),
            dma((2, chips - 1, slots)),
            dma((2, chips, slots)),
            dma((2, chips, slots)),
            dma((2, levels, fsdp)),
            dma((2, levels, fsdp)),
            dma((2, levels, fsdp)),
            dma((2, levels, fsdp)),
            dma((fsdp,)),
            dma((fsdp,)),
            dma((slots, ctx)),
            dma((8 + 3 * owned + slots,)),
        ],
        compiler_params=pltpu.CompilerParams(
            collective_id=0, has_side_effects=True, vmem_limit_bytes=60 * 2**20
        ),
        cost_estimate=pl.CostEstimate(flops=1000, bytes_accessed=1000, transcendentals=0),
    )(x, w, v)


def bits_of(count):
    return max(count.bit_length() - 1, 0)


def flip(count, value):
    return [(i, i ^ value) for i in range(count)]


def pick(array, index, axis):
    return lax.dynamic_index_in_dim(array, index, axis, keepdims=False)


def ordered(bit, mine, other, axis):
    first = jnp.where(bit == 0, mine, other)
    second = jnp.where(bit == 0, other, mine)
    return jnp.concatenate([first, second], axis=axis)


def after(value, *others):
    return lax.optimization_barrier((value, others))[0]


def add_low(mine, swapped):
    return (mine.astype(F32) + swapped.astype(F32)).astype(BF16)


def scatter_fsdp(total):
    return lax.psum_scatter(total, "fsdp", scatter_dimension=0, tiled=True)


def bar_signal(where):
    pl.semaphore_signal(
        pltpu.get_barrier_semaphore(), inc=1, device_id=where, device_id_type=pl.DeviceIdType.MESH
    )


def remote_copy(source, target, send, recv, where):
    return pltpu.make_async_remote_copy(
        src_ref=source,
        dst_ref=target,
        send_sem=send,
        recv_sem=recv,
        device_id=where,
        device_id_type=pl.DeviceIdType.MESH,
    )


def line_gather(chips, c, f, mine, slot, share, sems, core_sems):
    z, core = c // 2, lax.rem(c, 2)
    partner = 2 * z + 1 - core
    send, recv = sems
    core_send, core_recv = core_sems

    def passing(side, s):
        sign = 1 - 2 * side
        chip = z - sign * s
        source = mine if s == 0 else slot(chip)
        return remote_copy(
            source, slot(chip), send.at[side, s], recv.at[side, s], (c + 2 * sign, f)
        )

    def arrival(side, s):
        block = slot(z - (1 - 2 * side) * (s + 1))
        return remote_copy(block, block, send.at[side, s], recv.at[side, s], (partner, f))

    def sends(side, s):
        return (z - s >= 0) & (z < chips - 1) if side == 0 else (z + s < chips) & (z > 0)

    def gets(side, s):
        return z - 1 - s >= 0 if side == 0 else z + 1 + s < chips

    def shared(side, s):
        chip = z - (1 - 2 * side) * (s + 1)
        return remote_copy(
            slot(chip), share(chip), core_send.at[side, s], core_recv.at[side, s], (partner, f)
        )

    def share_arrival(side, s):
        block = share(z - (1 - 2 * side) * (s + 1))
        sems = core_send.at[side, s], core_recv.at[side, s]
        return remote_copy(block, block, *sems, (partner, f))

    own_sems = core_send.at[0, chips - 1], core_recv.at[0, chips - 1]
    own_share = remote_copy(mine, share(z), *own_sems, (partner, f))

    def start():
        for side in range(2):

            @pl.when(sends(side, 0))
            def _(side=side):
                passing(side, 0).start()

        own_share.start()

    def step(s):
        for side in range(2):

            @pl.when(gets(side, s))
            def _(side=side):
                arrival(side, s).wait_recv()
                shared(side, s).start()

            if s + 1 < chips - 1:

                @pl.when(sends(side, s + 1))
                def _(side=side):
                    passing(side, s + 1).start()

    def end():
        own_share.wait_send()
        remote_copy(share(z), share(z), *own_sems, (partner, f)).wait_recv()
        for s in range(chips - 1):
            for side in range(2):

                @pl.when(sends(side, s))
                def _(side=side, s=s):
                    passing(side, s).wait_send()

                @pl.when(gets(side, s))
                def _(side=side, s=s):
                    shared(side, s).wait_send()
                    share_arrival(side, s).wait_recv()

    return start, [functools.partial(step, s) for s in range(chips - 1)], end


def sum_kernel(ctx, fsdp, batches, *refs):
    levels, chips = bits_of(fsdp), ctx // 2
    pieces = refs[0:2]
    own_ref, mine_out, other_out, own_out, last_out = refs[2:7]
    rest = list(refs[7:])
    own_kept, own_low, beside = rest.pop(0), rest.pop(0), rest.pop(0)
    own_sent = [rest.pop(0) for _ in range(levels)]
    own_got = [rest.pop(0) for _ in range(levels)]
    z_sent, z_got = rest.pop(0), rest.pop(0)
    op_send, op_recv, zs_send, zs_recv, zg_send, zg_recv = (rest.pop(0) for _ in range(6))
    zc_send, zc_recv, og_send, og_recv, oc_send, oc_recv, far_send, far_recv, local = (
        rest.pop(0) for _ in range(9)
    )
    c, f = lax.axis_index("ctx"), lax.axis_index("fsdp")
    z, core = c // 2, lax.rem(c, 2)
    partner = 2 * z + 1 - core
    far = lax.rem(c + ctx // 2, ctx)
    rows = own_low.shape[0]
    chunk = z_sent.shape[-1]
    width = chunk * chips // 2
    parts = chips // 2
    strip = 16 if rows % 16 == 0 else 8

    def own_bit(bit):
        return lax.rem(f // (1 << bit), 2)

    def strips(work):
        def body(i, carry):
            work(pl.ds(pl.multiple_of(i * strip, strip), strip))
            return carry

        lax.fori_loop(0, rows // strip, body, 0)

    bar_signal((partner, f))
    bar_signal((far, f))
    for bit in range(levels):
        bar_signal((c, other_index(f, 1 << bit)))

    @pl.when(z > 0)
    def _():
        bar_signal((c - 2, f))

    @pl.when(z < chips - 1)
    def _():
        bar_signal((c + 2, f))

    neighbours = (z > 0).astype(jnp.int32) + (z < chips - 1).astype(jnp.int32)
    pl.semaphore_wait(pltpu.get_barrier_semaphore(), levels + 2 + neighbours)

    def order(q):
        return [(q + i) % levels for i in range(levels)]

    def place_of(q, flipped, free):
        bits = order(q)
        first = own_bit(bits[0])
        total = (1 - first if flipped else first) * (1 << bits[0])
        for i, bit in enumerate(bits[1:]):
            total += ((free >> i) & 1) * (1 << bit)
        return total

    def kept_index(q, step, flipped, free):
        bits = order(q)
        total = 0
        for i, bit in enumerate(bits[1:]):
            mine = own_bit(bit)
            if i + 1 < step:
                value = mine
            elif i + 1 == step:
                value = 1 - mine if flipped else mine
            else:
                value = (free >> (i - step)) & 1
            total += value * (1 << i)
        return total

    def across(step, q):
        return (c, other_index(f, 1 << order(q)[step]))

    def own_copy(step):
        return remote_copy(
            own_sent[step], own_got[step], op_send.at[step], op_recv.at[step], across(step, 0)
        )

    def own_begin():
        for free in range(fsdp // 2):
            there, here = place_of(0, True, free), place_of(0, False, free)

            def work(at, free=free, there=there, here=here):
                own_sent[0][free, at, :] = own_ref[there, at, :]
                own_kept[free, at, :] = own_ref[here, at, :].astype(F32)

            strips(work)
        own_copy(0).start()

    def later(step, kept_ref, got_ref, sent_ref, q):
        for free in range(fsdp >> (step + 2)):
            there, here = (kept_index(q, step + 1, flipped, free) for flipped in (True, False))
            mine = own_bit(order(q)[step + 1])
            there_got, here_got = free * 2 + 1 - mine, free * 2 + mine

            def work(at, free=free):
                value = kept_ref[there, at, :] + got_ref[there_got, at, :].astype(F32)
                sent_ref[free, at, :] = value.astype(BF16)
                kept_ref[here, at, :] += got_ref[here_got, at, :].astype(F32)

            strips(work)

    def last(kept_ref, got_ref, q, place):
        def work(at):
            place(at, kept_ref[kept_index(q, levels, False, 0), at, :] + got_ref[0, at, :].astype(F32))

        strips(work)

    def own_step(step):
        own_copy(step).wait_recv()
        if step + 1 < levels:
            later(step, own_kept, own_got[step], own_sent[step + 1], 0)
            own_copy(step + 1).start()
            return

        def place(at, value):
            own_low[at, :] = value[:, : head + tail].astype(BF16)
            beside[at, :] = value[:, head + tail :]

        last(own_kept, own_got[step], 0, place)
        for copy in far_copies:
            copy.start()
        own_start()

    head = own_out.shape[2]
    tail = last_out.shape[2]
    far_copies = [
        remote_copy(
            own_low.at[:, pl.ds(head, tail)], last_out.at[1], far_send.at[0], far_recv.at[0], (far, f)
        ),
        pltpu.make_async_copy(own_low.at[:, pl.ds(head, tail)], last_out.at[0], local.at[0]),
        pltpu.make_async_copy(own_low.at[:, pl.ds(0, head)], own_out.at[c], local.at[1]),
    ]
    own_start, own_steps, own_end = line_gather(
        chips,
        c,
        f,
        own_low.at[:, pl.ds(0, head)],
        lambda chip: own_out.at[2 * chip + core],
        lambda chip: own_out.at[2 * chip + core],
        (og_send, og_recv),
        (oc_send, oc_recv),
    )

    def total_of(j, b, at):
        q = j // parts
        start = b * width + (j % parts) * chunk
        stop = start + chunk
        units, room = pieces[q].shape[1], beside.shape[1] // 2
        found = []
        if start < units:
            found.append(pieces[q][at, start : min(stop, units)].astype(F32))
        if stop > units:
            first = max(start, units) - units + q * room
            found.append(beside[at, first : stop - units + q * room])
        return found[0] if len(found) == 1 else jnp.concatenate(found, axis=1)

    def z_copy(side, i, b):
        return remote_copy(
            z_sent.at[side, b, i],
            z_got.at[side, b, i],
            zs_send.at[side, b, i],
            zs_recv.at[side, b, i],
            (c + 2 * (1 - 2 * side), f),
        )

    def z_last(side, chip):
        return chips - 1 - chip if side == 0 else chip

    def z_step(turn, b):
        for chip in range(chips):

            @pl.when(z == chip)
            def _(chip=chip):
                for side in range(2):
                    j_of = (lambda i: chips - 1 - i) if side == 0 else (lambda i: i)
                    begun = chip if side == 0 else chips - 1 - chip
                    i = turn - begun
                    sends = z_last(side, chip)
                    if begun > 0 and 0 <= i <= sends and i < chips - 1:
                        z_copy(side, i, b).wait_recv()
                    if 0 <= i < sends:
                        if i > 0:
                            z_copy(side, i - 1, b).wait_send()

                        def work(at, side=side, i=i, j=j_of(i), begun=begun):
                            value = total_of(j, b, at)
                            if begun > 0:
                                value += z_got[side, b, i, at, :].astype(F32)
                            z_sent[side, b, i, at, :] = value.astype(BF16)

                        strips(work)
                        z_copy(side, i, b).start()

    def chunk_of(ref, chip, b):
        start = pl.multiple_of(b * width + lax.rem(chip, parts) * chunk, 128)
        return ref.at[chip // parts, :, pl.ds(start, chunk)]

    gathers = []
    for b in range(batches):
        gathers.append(
            line_gather(
                chips,
                c,
                f,
                chunk_of(mine_out, z, b),
                lambda chip, b=b: chunk_of(mine_out, chip, b),
                lambda chip, b=b: chunk_of(other_out, chip, b),
                (zg_send.at[:, b], zg_recv.at[:, b]),
                (zc_send.at[:, b], zc_recv.at[:, b]),
            )
        )

    def finish(b):
        for j in range(chips):

            @pl.when(z == j)
            def _(j=j):
                def work(at):
                    value = total_of(j, b, at)
                    if j > 0:
                        value += z_got[0, b, chips - 1 - j, at, :].astype(F32)
                    if j < chips - 1:
                        value += z_got[1, b, j, at, :].astype(F32)
                    start = b * width + (j % parts) * chunk
                    mine_out[j // parts, at, pl.ds(start, chunk)] = value.astype(BF16)

                strips(work)

        gathers[b][0]()

    own_begin()
    waiting = []

    def one_more():
        if waiting:
            waiting.pop(0)()

    def batch(b):
        for i in range(chips):
            z_step(i, b)
            one_more()
        finish(b)
        waiting.extend(gathers[b][1])

    for b in range(batches - 1):
        batch(b)
    for step in range(levels):
        own_step(step)
        one_more()
    waiting.extend(own_steps)
    batch(batches - 1)
    while waiting:
        one_more()

    far_copies[0].wait()
    far_copies[1].wait()
    far_copies[2].wait()
    own_end()
    for step in range(levels):
        own_copy(step).wait_send()
    for b in range(batches):
        gathers[b][2]()
        for chip in range(chips):

            @pl.when(z == chip)
            def _(chip=chip, b=b):
                for side in range(2):
                    if z_last(side, chip):
                        z_copy(side, z_last(side, chip) - 1, b).wait_send()


def sum_grads(ctx, fsdp, pieces, own, head, tail):
    levels, chips = bits_of(fsdp), ctx // 2
    rows, units = pieces[0].shape
    rest = own.shape[-1] - head - tail
    whole = units + rest // 2
    batches = max(n for n in range(1, 3) if whole % n == 0 and 2 * whole // n % (chips * 128) == 0)
    width = whole // batches
    chunk = 2 * width // chips
    own_width = own.shape[-1]
    vmem = pl.BlockSpec(memory_space=pltpu.VMEM)
    dma = pltpu.SemaphoreType.DMA
    steps = [fsdp >> (i + 1) for i in range(levels)]
    result = jax.ShapeDtypeStruct((2, rows, whole), BF16)
    mine, other, own_all, last = pl.pallas_call(
        functools.partial(sum_kernel, ctx, fsdp, batches),
        in_specs=[vmem] * 3,
        out_specs=[vmem] * 4,
        out_shape=[
            result,
            result,
            jax.ShapeDtypeStruct((ctx, rows, head), BF16),
            jax.ShapeDtypeStruct((2, rows, tail), BF16),
        ],
        scratch_shapes=[
            pltpu.VMEM((fsdp // 2, rows, own_width), F32),
            pltpu.VMEM((rows, head + tail), BF16),
            pltpu.VMEM((rows, rest), F32),
        ]
        + [pltpu.VMEM((n, rows, own_width), BF16) for n in steps * 2]
        + [pltpu.VMEM((2, batches, chips - 1, rows, chunk), BF16)] * 2
        + [dma((levels,))] * 2
        + [dma((2, batches, chips - 1))] * 4
        + [dma((2, batches, chips))] * 2
        + [dma((2, chips - 1))] * 2
        + [dma((2, chips))] * 2
        + [dma((1,))] * 2
        + [dma((6,))],
        compiler_params=pltpu.CompilerParams(
            collective_id=1, has_side_effects=True, vmem_limit_bytes=60 * 2**20
        ),
        cost_estimate=pl.CostEstimate(flops=1000, bytes_accessed=1000, transcendentals=0),
    )(*pieces, own)

    return mine, other, own_all, last


def swap_cores(mine, ctx):
    return lax.ppermute(mine, "ctx", flip(ctx, 1))


def norm_parts(rows, axis):
    middle = jnp.mean(rows, axis=axis, keepdims=True)
    centred = rows - middle
    spread = jnp.mean(centred * centred, axis=axis, keepdims=True)
    inverse = lax.rsqrt(spread + NORM_EPS)
    return centred * inverse, inverse


def norm_back(grad, unit, inverse, gain):
    inner = grad * gain
    mean_inner = jnp.mean(inner, axis=1, keepdims=True)
    mean_cross = jnp.mean(inner * unit, axis=1, keepdims=True)
    rows = inverse * (inner - mean_inner - unit * mean_cross)
    return rows, jnp.sum(grad * unit, axis=(0, 2)), jnp.sum(grad, axis=(0, 2))


def adamw(weight, first, second, grad, rate, decay):
    moment = BETA_ONE * first.astype(F32) + (1.0 - BETA_ONE) * grad
    square = BETA_TWO * second + (1.0 - BETA_TWO) * grad * grad
    corrected = moment / (1.0 - BETA_ONE**STEP)
    scaled = square / (1.0 - BETA_TWO**STEP)
    new_weight = weight - rate * (corrected / (jnp.sqrt(scaled) + ADAM_EPS) + decay * weight)
    return (moment, square, new_weight)


def update_kernel(units, regular, *refs):
    (w, first, second, dw, dfirst, dsecond, own, last, mine, other) = refs[:10]
    outs = refs[10:]
    core = lax.rem(lax.axis_index("ctx"), 2)
    width = (w.shape[1] - 2 * units) // 4
    quarter = width // 4
    ctx = own.shape[0]
    dim = HEAD_DIM

    def halves(q, start, size):
        here = mine[q, :, start : start + size].astype(F32)
        there = other[q, :, start : start + size].astype(F32)
        return jnp.where(core == 0, here, there), jnp.where(core == 0, there, here)

    def both(q, start, size):
        return jnp.concatenate(halves(q, start, size), axis=1)

    heads = []
    for part in range(3):
        for i in range(regular):
            for c in range(ctx):
                column = (i * 3 + part) * dim
                heads.append(own[c, :, column : column + dim].astype(F32))
        column = part * dim
        heads.append(
            last[0, :, column : column + dim].astype(F32)
            + last[1, :, column : column + dim].astype(F32)
        )
    out = [halves(q, units, quarter) for q in range(2)]
    heads += [out[0][0], out[1][0], out[0][1], out[1][1]]
    grad = jnp.concatenate(heads, axis=1)

    def put(targets, cols, values):
        for target, value in zip(targets, values):
            target[:, cols] = value

    cols = slice(0, 4 * width)
    put(outs[:3], cols, adamw(w[:, cols], first[:, cols], second[:, cols], grad, 0.03, 0.1))
    cols = slice(4 * width, w.shape[1])
    grad = both(0, 0, units)
    put(outs[:3], cols, adamw(w[:, cols], first[:, cols], second[:, cols], grad, 0.03, 0.1))
    grad = both(1, 0, units)
    put(outs[3:], slice(None), adamw(dw[...], dfirst[...], dsecond[...], grad, 0.02, 0.1))


def update(rows_state, down_state, own, last, mine, other, units, regular):
    rows = rows_state[0].shape[0]
    strip = 16 if rows % 16 == 0 else 8

    def flat(array):
        return pl.BlockSpec((strip, array.shape[1]), lambda i: (i, 0))

    def deep(array):
        return pl.BlockSpec((array.shape[0], strip, array.shape[2]), lambda i: (0, i, 0))

    states, sums = [*rows_state, *down_state], [own, last, mine, other]
    results = [rows_state[0]] * 3 + [down_state[0]] * 3
    return pl.pallas_call(
        functools.partial(update_kernel, units, regular),
        grid=(rows // strip,),
        in_specs=[flat(a) for a in states] + [deep(a) for a in sums],
        out_specs=[flat(a) for a in results],
        out_shape=[jax.ShapeDtypeStruct(a.shape, F32) for a in results],
        compiler_params=pltpu.CompilerParams(vmem_limit_bytes=56 * 2**20),
        cost_estimate=pl.CostEstimate(flops=1000, bytes_accessed=1000, transcendentals=0),
    )(*states, *sums)


def body(
    ctx,
    fsdp,
    tokens,
    cotangent,
    lengths,
    w_rows,
    rows_first,
    rows_second,
    w_down,
    down_first,
    down_second,
    vectors,
    vec_first,
    vec_second,
):
    tok, slots, width = tokens.shape
    dim = HEAD_DIM
    regular = HEADS // ctx
    owned = regular + 1
    share = width // fsdp
    c = lax.axis_index("ctx")
    core = c % 2
    late = (c >= ctx // 2).astype(jnp.int32)
    half = FF // 2

    def my_half(array):
        return lax.dynamic_slice_in_dim(array, core * half, half, 1)

    x_low = tokens.transpose(1, 2, 0)
    vec_part = jnp.pad(vectors.astype(BF16).T, ((0, 0), (0, 128 - vectors.shape[0])))
    act_all, qkv_all, head_w, up_mine, up_other, vec_low = gather_first(
        ctx, fsdp, regular, x_low, w_rows, vec_part
    )
    head_w = head_w.reshape(width, 4 * width)
    up_mine, up_other = up_mine.reshape(width, half), up_other.reshape(width, half)
    vec_low = vec_low.reshape(width, 128)
    down_mine, vec_low = lax.optimization_barrier((my_half(w_down.T).astype(BF16), vec_low))
    down_mine = lax.all_gather(down_mine, "fsdp", axis=0, tiled=True)
    vec = [vec_low[:, i : i + 1].astype(F32) for i in range(12)]
    up_bias = vec_low[:, 8:12].T.astype(F32).reshape(1, FF)

    qkv_all = qkv_all.reshape(slots, 3, owned, dim, ctx * tok)
    far = (c + ctx // 2) % ctx

    def to_rows(array, *gate):
        feat = array.shape[2]
        got = lax.all_to_all(array, "ctx", 0, 0)
        got = after(got, *gate) if gate else got
        return got.transpose(1, 0, 2, 3).reshape(regular * ctx, feat, tok)

    def last_to_rows(array, *gate):
        mine = pick(array, c, 0)
        got = lax.ppermute(pick(array, far, 0), "ctx", flip(ctx, ctx // 2))
        got = after(got, *gate) if gate else got
        return jnp.where(late == 0, mine, got), jnp.where(late == 0, got, mine)

    def to_send(array):
        return array.reshape(regular, ctx, dim, tok).transpose(1, 0, 2, 3)

    def attend_slot(s, *gate):
        lens = after(jnp.repeat(lengths[s : s + 1], regular), *gate)
        return (lens, qkv_all, s, *attend(lens, qkv_all, s, tok))

    results = [attend_slot(0)]
    results.append(attend_slot(1, results[0][3]))
    rows = [to_rows(results[0][4])]
    last_qkv = jnp.where(late == 0, qkv_all[:1, :, regular:], qkv_all[1:, :, regular:])
    last_len = after(lax.dynamic_slice_in_dim(lengths, late, 1, 0), results[1][3], rows[0])
    results.append((last_len, last_qkv, 0, *attend(last_len, last_qkv, 0, tok)))
    rows.append(to_rows(results[1][4]))
    down_mine = after(down_mine, results[2][3], *rows)
    down_other = swap_cores(down_mine, ctx)
    last_rows = last_to_rows(results[2][4])
    att = [jnp.concatenate([rows[s], last_rows[s]]).reshape(width, tok) for s in range(slots)]
    att = jnp.stack(att)

    x = x_low.astype(F32)
    out_w = head_w[:, 3 * width :]
    mid = x + jnp.einsum("de,sdt->set", out_w, att, preferred_element_type=F32) + vec[4]
    unit_two, inverse_two = norm_parts(mid, 1)
    act_two = (unit_two * vec[5] + vec[6]).astype(BF16)

    pos = c * tok + jnp.arange(tok, dtype=jnp.int32)
    valid = pos[None, None, :] < lengths[:, None, None]
    g_low = jnp.where(valid, cotangent.transpose(1, 2, 0), jnp.zeros((), BF16))
    g = g_low.astype(F32)

    bias_mine = lax.dynamic_slice_in_dim(up_bias, core * half, half, 1)
    bias_other = lax.dynamic_slice_in_dim(up_bias, (1 - core) * half, half, 1)
    y_other, ga_other, dup_other, ddown_other, db_other = mlp(
        act_two, g_low, up_other, down_other, bias_other
    )
    y_mine, ga_mine, dup_mine, ddown_mine, db_mine = mlp(
        act_two, g_low, up_mine, down_mine, bias_mine
    )
    output = (mid + (y_mine + y_other + vec[7])).astype(BF16).transpose(2, 0, 1)

    up_swapped, down_swapped = swap_cores(dup_other, ctx), swap_cores(ddown_other, ctx)
    up_total = add_low(dup_mine, up_swapped)
    up_part = scatter_fsdp(up_total)
    ga_mine = after(ga_mine, up_total)

    grad_mid, gain_two, shift_two = norm_back(ga_mine + ga_other, unit_two, inverse_two, vec[5])
    grad_mid = g + grad_mid
    grad_attn = grad_mid.astype(BF16)
    grad_att = jnp.einsum("de,set->sdt", out_w, grad_attn, preferred_element_type=F32).astype(BF16)
    down_part = scatter_fsdp(add_low(after(ddown_mine, grad_att), down_swapped))
    grad_attn_later = after(grad_attn, grad_att)
    grad_att = grad_att.reshape(slots, HEADS, dim, tok)
    last = jnp.repeat(grad_att[:, -1], ctx // slots, axis=0)[:, None]
    first_pairs = lax.all_to_all(to_send(grad_att[0, :-1]), "ctx", 0, 0)
    other_pairs = lax.all_to_all(
        after(jnp.concatenate([to_send(grad_att[1, :-1]), last], axis=1), first_pairs), "ctx", 0, 0
    )

    quarter = width // 4
    spread = jnp.pad(
        grad_attn_later.reshape(slots, 4, quarter, tok),
        ((0, 0), (0, 0), (0, -quarter % 128), (0, 0)),
    )
    out_grad = jnp.einsum("sdt,sket->kde", att, spread, preferred_element_type=F32).astype(BF16)
    out_grad = out_grad.reshape(2, 2, fsdp, share, spread.shape[2])

    def out_half(which):
        return pick(out_grad, which, 0).reshape(2, width, spread.shape[2])

    out_mine, out_swapped = out_half(core), swap_cores(out_half(1 - core), ctx)
    out_total = add_low(out_mine, out_swapped)
    first_heads = attend_back(*results[0][:4], results[0][5], first_pairs)
    last_heads = attend_back(
        *results[2][:4], results[2][5], after(other_pairs[:, -1:], first_heads)
    )
    other_heads = attend_back(
        *results[1][:4], results[1][5], after(other_pairs[:, :-1], last_heads, up_part)
    )
    grad_heads = [first_heads, other_heads, last_heads]

    feat = 3 * dim
    own_sum = own_grad(
        late,
        act_all,
        grad_heads[0].reshape(ctx, regular * feat, tok),
        grad_heads[1].reshape(ctx, regular * feat, tok),
        grad_heads[2].reshape(ctx, feat, tok),
    )
    own_sum = own_sum.astype(BF16)
    own_sum = jnp.concatenate(
        [
            jnp.pad(part, ((0, 0), (0, -part.shape[1] % 128)))
            for part in (own_sum[:, : regular * feat], own_sum[:, regular * feat :])
        ]
        + [out_total[0], out_total[1]],
        axis=1,
    )
    head_columns = regular * feat + -regular * feat % 128
    blocks = (fsdp, share)
    sum_mine, sum_other, own_all, last = sum_grads(
        ctx,
        fsdp,
        [up_part, down_part],
        own_sum.reshape(*blocks, own_sum.shape[1]),
        head_columns,
        feat + -feat % 128,
    )
    first_rows, other_rows = to_rows(first_heads), to_rows(other_heads, sum_mine)
    last_rows = last_to_rows(last_heads, sum_mine)
    grad_qkv = []
    for s, rows in enumerate((first_rows, other_rows)):
        rows = jnp.concatenate([rows, last_rows[s]])
        rows = rows.reshape(HEADS, 3, dim, tok).transpose(1, 0, 2, 3)
        grad_qkv.append(rows.reshape(3 * width, tok))
    grad_qkv = jnp.stack(grad_qkv)
    grad_one = jnp.einsum(
        "de,set->sdt", head_w[:, : 3 * width], grad_qkv, preferred_element_type=F32
    )

    unit_one, inverse_one = norm_parts(x, 1)
    grad_in, gain_one, shift_one = norm_back(grad_one, unit_one, inverse_one, vec[0])
    grad_tokens = (grad_mid + grad_in).astype(BF16)

    bias_qkv = jnp.sum(grad_qkv.astype(F32), axis=(0, 2))
    vec_grad = jnp.stack(
        [
            gain_one,
            shift_one,
            bias_qkv[:width],
            bias_qkv[2 * width :],
            jnp.sum(grad_attn.astype(F32), axis=(0, 2)),
            gain_two,
            shift_two,
            jnp.sum(g, axis=(0, 2)),
        ]
    )
    bias_up = ordered(core, db_mine, db_other, 1).reshape(4, width)
    vec_grad = jnp.concatenate([vec_grad, bias_up], axis=0).reshape(12, fsdp, share)
    f = lax.axis_index("fsdp")
    vec_sum = pick(vec_grad, f, 1)
    for value in range(1, fsdp):
        vec_sum = vec_sum + lax.ppermute(pick(vec_grad, f ^ value, 1), "fsdp", flip(fsdp, value))
    for level in range(bits_of(ctx)):
        vec_sum = vec_sum + lax.ppermute(vec_sum, "ctx", flip(ctx, 2**level))

    rows_state = (w_rows, rows_first, rows_second)
    down_state = (w_down.T, down_first.T, down_second.T)
    updated = update(
        rows_state, down_state, own_all, last, sum_mine, sum_other, half, regular
    )
    rows_out, down_out = updated[:3], tuple(part.T for part in updated[3:])
    vec_out = adamw(vectors, vec_first, vec_second, vec_sum, 0.3, 0.0)
    return (output, grad_tokens.transpose(2, 0, 1), *rows_out, *down_out, *vec_out)


def solution(mesh):
    placed = (
        P("ctx", "fsdp", None),
        P("ctx", "fsdp", None),
        P("fsdp"),
        P("fsdp", None),
        P("fsdp", None),
        P("fsdp", None),
        P(None, "fsdp"),
        P(None, "fsdp"),
        P(None, "fsdp"),
        P(None, "fsdp"),
        P(None, "fsdp"),
        P(None, "fsdp"),
    )
    return jax.shard_map(
        functools.partial(body, mesh.shape["ctx"], mesh.shape["fsdp"]),
        mesh=mesh,
        in_specs=placed,
        out_specs=placed[:2] + placed[3:6] + placed[6:9] + placed[9:12],
        check_vma=False,
    )
```

profile of v0, /device:TPU:0, one launch (start us, length us, event | category | flops | bytes accessed | tf_op | source)
XLA Modules:
  0.0 582.0 jit_solution(14276077127009773641)
XLA Ops:
  8.1 2.8 fusion.17
  11.6 108.9 %shard_map.203 = (bf16[2,8,1088,256]{3,2,1,0:T(8,128)(2,1)}, bf16[2,576,2048]{2,1,0:T(8,128)(2,1)}, bf16[4,272,4352]{2,1,0:T(8,128)(2,1)}, bf16[4,272,2176]{2,1,...) custom-call(bf16[2,1088,256]{2,1,0:T(8,128)(2,1)} %bitcast.157, f32[272,8704]{1,0:T(8,128)} %refs_0_.1, ...), custom_call_target="tpu_custom_call" | custom-call | flops 1000 | bytes 1000 | tf_op jit(solution)/shard_map/pallas_call | solution.py:833
  121.8 12.5 %shard_map.204 = (f32[2,64,2048]{2,1,0:T(8,128)S(1)}, bf16[8,2,64,256]{3,2,1,0:T(8,128)(2,1)}, f32[2,1,2048]{2,1,0:T(1,128)S(1)}) custom-call(s32[2]{0:T(128)S(1)} %reshape.210.lens_ref, bf16[2,3,3,64,2048]{4,3,2,1,0:T(8,128)(2,1)} %bitcast.144, bf16[2,3,3,64,2048]{4,3,2,1,0:T(8,128)(2,1)} %bitcast.145, bf16[2,3,3,64,2048]{4,3,2,1,0:T(8,128)(2,1)} %bitcast.146), custom_call_target="tpu_custom_call" | custom-call | flops 1000 | bytes 1000 | tf_op jit(solution)/shard_map/pallas_call | solution.py:114
  135.3 6.1 %all-to-all-start = ((bf16[8,2,64,256]{3,2,1,0:T(8,128)(2,1)}), bf16[8,2,64,256]{3,2,1,0:T(8,128)(2,1)S(1)}, u32[]{:S(2)}, u32[]{:S(2)}) async-start(bf16[8,2,64,256]{3,2,1,0:T(8,128)(2,1)} %get-tuple-element.60), calls=%async_computation | async-start | bytes 1048576 | tf_op jit(solution)/shard_map/all_to_all | solution.py:1469
  142.0 12.1 %shard_map.205 = (f32[2,64,2048]{2,1,0:T(8,128)S(1)}, bf16[8,2,64,256]{3,2,1,0:T(8,128)(2,1)}, f32[2,1,2048]{2,1,0:T(1,128)S(1)}) custom-call(s32[2]{0:T(128)S(1)} %reshape.213.lens_ref, bf16[2,3,3,64,2048]{4,3,2,1,0:T(8,128)(2,1)} %bitcast.147, bf16[2,3,3,64,2048]{4,3,2,1,0:T(8,128)(2,1)} %bitcast.148, bf16[2,3,3,64,2048]{4,3,2,1,0:T(8,128)(2,1)} %bitcast.149), custom_call_target="tpu_custom_call" | custom-call | flops 1000 | bytes 1000 | tf_op jit(solution)/shard_map/pallas_call | solution.py:114
  154.2 2.6 all-to-all-done
  156.7 4.2 all-to-all-start.1
  161.0 1.5 slice_select_fusion.q_ref.k_ref.v_ref
  162.5 7.0 %shard_map.206 = (f32[1,64,2048]{2,1,0:T(8,128)S(1)}, bf16[8,1,64,256]{3,2,1,0:T(8,128)(2,1)S(1)}, f32[1,1,2048]{2,1,0:T(1,128)S(1)}) custom-call(s32[1]{0:T(128)} %get-tuple-element.64.lens_ref, bf16[1,3,1,64,2048]{4,3,2,1,0:T(8,128)(2,1)S(1)} %slice_select_fusion.q_ref.k_ref.v_ref, bf16[1,3,1,64,2048]{4,3,2,1,0:T(8,128)(2,1)S(1)} %slice_select_fusion.q_ref.k_ref.v_ref, ...), custom_call_target="tpu_custom_call" | custom-call | flops 1000 | bytes 1000 | tf_op jit(solution)/shard_map/pallas_call | solution.py:114
  169.5 6.7 %all-to-all-done.1 = bf16[8,2,64,256]{3,2,1,0:T(8,128)(2,1)} async-done(((bf16[8,2,64,256]{3,2,1,0:T(8,128)(2,1)}), bf16[8,2,64,256]{3,2,1,0:T(8,128)(2,1)}, u32[]{:S(2)}, u32[]{:S(2)}) %all-to-all-start.1) | async-done | bytes 524320 | tf_op jit(solution)/shard_map/all_to_all | solution.py:1469
  176.3 1.9 copy.66
  178.1 1.4 all-gather.2.cloned.1.call-done.down_ref
  180.9 2.5 convert_reduce_fusion.2
  184.6 2.4 collective-permute-start
  187.1 2.7 collective-permute-done
  191.7 4.9 fusion.40
  197.0 1.4 add_convert_fusion.3.a_ref
  198.4 25.2 %shard_map.208 = (f32[2,1088,256]{2,1,0:T(8,128)}, f32[2,1088,256]{2,1,0:T(8,128)}, bf16[1088,2176]{1,0:T(8,128)(2,1)}, bf16[1088,2176]{1,0:T(8,128)(2,1)}, f32[1,2176]{1,0:T(1,128)}) custom-call(bf16[2,1088,256]{2,1,0:T(8,128)(2,1)} %add_convert_fusion.3.a_ref, bf16[2,1088,256]{2,1,0:T(8,128)(2,1)} %get-tuple-element.123.g_ref, ...), custom_call_target="tpu_custom_call" | custom-call | flops 1000 | bytes 1000 | tf_op jit(solution)/shard_map/pallas_call | solution.py:369
  223.6 25.4 %shard_map.207 = (f32[2,1088,256]{2,1,0:T(8,128)}, f32[2,1088,256]{2,1,0:T(8,128)}, bf16[1088,2176]{1,0:T(8,128)(2,1)}, bf16[1088,2176]{1,0:T(8,128)(2,1)}, f32[1,2176]{1,0:T(1,128)}) custom-call(bf16[2,1088,256]{2,1,0:T(8,128)(2,1)} %add_convert_fusion.3.a_ref, bf16[2,1088,256]{2,1,0:T(8,128)(2,1)} %get-tuple-element.123.g_ref, ...), custom_call_target="tpu_custom_call" | custom-call | flops 1000 | bytes 1000 | tf_op jit(solution)/shard_map/pallas_call | solution.py:369
  249.0 5.7 add_convert_fusion.1
  255.3 4.9 multiply_reduce_fusion
  261.5 5.1 convolution_convert_fusion
  266.7 3.5 add_convert_fusion
  270.2 1.3 fusion.37
  272.3 5.1 all-to-all-start.2
  279.3 13.5 %all-to-all-done.2.grad_ref = bf16[8,2,64,256]{3,2,1,0:T(8,128)(2,1)S(1)} async-done(((bf16[8,2,64,256]{3,2,1,0:T(8,128)(2,1)}), bf16[8,2,64,256]{3,2,1,0:T(8,128)(2,1)S(1)}, u32[]{:S(2)}, u32[]{:S(2)}) %all-to-all-start.2) | async-done | bytes 524320 | tf_op jit(solution)/shard_map/all_to_all | solution.py:1533
  292.8 4.4 all-to-all-start.4
  297.2 1.4 copy-done.1
  298.6 18.5 %shard_map.209 = bf16[8,2,192,256]{3,2,1,0:T(8,128)(2,1)} custom-call(s32[2]{0:T(128)S(1)} %reshape.210.lens_ref, bf16[2,3,3,64,2048]{4,3,2,1,0:T(8,128)(2,1)} %bitcast.151, bf16[2,3,3,64,2048]{4,3,2,1,0:T(8,128)(2,1)} %bitcast.152, bf16[2,3,3,64,2048]{4,3,2,1,0:T(8,128)(2,1)} %bitcast.153, f32[2,64,2048]{2,1,0:T(8,128)S(1)} %copy-done.1, ...), custom_call_target="tpu_custom_call" | custom-call | flops 1000 | bytes 1000 | tf_op jit(solution)/shard_map/pallas_call | solution.py:220
  318.2 4.3 all-to-all-start.3
  322.5 3.2 bitcast_convert_fusion
  325.7 2.1 constant_dynamic-slice_fusion.4
  330.3 9.1 %shard_map.210 = bf16[8,1,192,256]{3,2,1,0:T(8,128)(2,1)S(1)} custom-call(s32[1]{0:T(128)} %get-tuple-element.64.lens_ref, bf16[1,3,1,64,2048]{4,3,2,1,0:T(8,128)(2,1)S(1)} %slice_select_fusion.q_ref.k_ref.v_ref, bf16[1,3,1,64,2048]{4,3,2,1,0:T(8,128)(2,1)S(1)} %slice_select_fusion.q_ref.k_ref.v_ref, ...), custom_call_target="tpu_custom_call" | custom-call | flops 1000 | bytes 1000 | tf_op jit(solution)/shard_map/pallas_call | solution.py:220
  340.6 18.9 %shard_map.211 = bf16[8,2,192,256]{3,2,1,0:T(8,128)(2,1)} custom-call(s32[2]{0:T(128)S(1)} %reshape.213.lens_ref, bf16[2,3,3,64,2048]{4,3,2,1,0:T(8,128)(2,1)} %bitcast.154, bf16[2,3,3,64,2048]{4,3,2,1,0:T(8,128)(2,1)} %bitcast.155, bf16[2,3,3,64,2048]{4,3,2,1,0:T(8,128)(2,1)} %bitcast.156, f32[2,64,2048]{2,1,0:T(8,128)S(1)} %get-tuple-element.63.o_ref, ...), custom_call_target="tpu_custom_call" | custom-call | flops 1000 | bytes 1000 | tf_op jit(solution)/shard_map/pallas_call | solution.py:220
  360.3 4.7 all-to-all-start.5
  365.5 1.9 fusion.1
  367.5 2.9 collective-permute-start.3
  370.4 1.5 copy.75
  372.0 13.0 %shard_map.212 = f32[1088,576]{1,0:T(8,128)} custom-call(s32[1]{0:T(128)} %bitcast.37.late_ref, bf16[2,8,1088,256]{3,2,1,0:T(8,128)(2,1)} %get-tuple-element.89.first_ref.second_ref, bf16[2,8,1088,256]{3,2,1,0:T(8,128)(2,1)} %get-tuple-element.89.first_ref.second_ref, bf16[8,384,256]{2,1,0:T(8,128)(2,1)} %bitcast.38.first_grad_ref, ...), custom_call_target="tpu_custom_call" | custom-call | flops 1000 | bytes 1000 | tf_op jit(solution)/shard_map/pallas_call | solution.py:283
  385.0 1.9 convert_element_type.117
  387.2 1.8 pad_maximum_fusion.1.refs_2_
  389.0 120.7 %shard_map.213 = (bf16[2,272,2560]{2,1,0:T(8,128)(2,1)}, bf16[2,272,2560]{2,1,0:T(8,128)(2,1)}, bf16[8,272,384]{2,1,0:T(8,128)(2,1)}, bf16[2,272,256]{2,1,0:T(8,128)(2,1)}) custom-call(bf16[272,2176]{1,0:T(8,128)(2,1)} %reduce-scatter.7.cloned.1.call-done.refs_0_, bf16[272,2176]{1,0:T(8,128)(2,1)} %reduce-scatter.9.cloned.1.call-done.refs_1_, ...), custom_call_target="tpu_custom_call" | custom-call | flops 1000 | bytes 1000 | tf_op jit(solution)/shard_map/pallas_call | solution.py:1292
  510.1 2.1 copy.79
  514.3 9.0 %fusion.13 = (f32[1088]{0:T(1024)S(1)}, f32[2,256]{1,0:T(2,128)}, f32[2,256]{1,0:T(2,128)}, f32[2,256,1088]{1,2,0:T(8,128)S(1)}) fusion(f32[2,256]{1,0:T(2,128)S(1)} %add_rsqrt_fusion, f32[2,256]{1,0:T(2,128)S(1)} %copy-done.28, bf16[256,2,1088]{0,2,1:T(8,128)(2,1)S(1)} %copy-done.11, f32[1088]{0:T(1024)S(1)} %get-tuple-element.114, ...), kind=kOutput, calls=%fused_computation.30 | convolution fusion | flops 3648157696 | bytes 13943296 | tf_op jit(solution)/shard_map/de,set->sdt/dot_general | solution.py:1595
  526.1 1.7 collective-permute-start.8
  527.8 36.4 %shard_map.214 = (f32[272,8704]{1,0:T(8,128)}, f32[272,8704]{1,0:T(8,128)}, f32[272,8704]{1,0:T(8,128)}, f32[272,4352]{1,0:T(8,128)}, f32[272,4352]{1,0:T(8,128)}, /*index=5*/f32[272,4352]{1,0:T(8,128)}) custom-call(f32[272,8704]{1,0:T(8,128)} %refs_0_.1, bf16[272,8704]{1,0:T(8,128)(2,1)} %refs_1_.1, f32[272,8704]{1,0:T(8,128)} %refs_2_.1, ...), custom_call_target="tpu_custom_call" | custom-call | flops 1000 | bytes 1000 | tf_op jit(solution)/shard_map/pallas_call | solution.py:1411
  565.5 3.8 collective-permute-done.10
  569.4 4.9 fusion.19
  (185 shorter events, 27.4 us)
Async XLA Ops:
  7.2 172.4 %all-gather.2.cloned.1.call-start = ((), (), s32[]{:S(2)}) async-start(), calls=%async_computation.8 | async-start | bytes 5918720 | tf_op jit(solution)/shard_map/all_gather | solution.py:1460
  11.6 109.0 %copy-start.34 = (s32[2]{0:T(128)S(1)}, s32[2]{0:T(128)}, u32[]{:S(2)}) copy-start(s32[2]{0:T(128)} %param.14) | copy-start | bytes 28
  135.3 21.4 %all-to-all-start = ((bf16[8,2,64,256]{3,2,1,0:T(8,128)(2,1)}), bf16[8,2,64,256]{3,2,1,0:T(8,128)(2,1)S(1)}, u32[]{:S(2)}, u32[]{:S(2)}) async-start(bf16[8,2,64,256]{3,2,1,0:T(8,128)(2,1)} %get-tuple-element.60), calls=%async_computation | async-start | bytes 1048576 | tf_op jit(solution)/shard_map/all_to_all | solution.py:1469
  156.7 19.5 %all-to-all-start.1 = ((bf16[8,2,64,256]{3,2,1,0:T(8,128)(2,1)}), bf16[8,2,64,256]{3,2,1,0:T(8,128)(2,1)}, u32[]{:S(2)}, u32[]{:S(2)}) async-start(bf16[8,2,64,256]{3,2,1,0:T(8,128)(2,1)} %get-tuple-element.66), calls=%async_computation.1 | async-start | bytes 1048576 | tf_op jit(solution)/shard_map/all_to_all | solution.py:1469
  160.9 179.6 %reduce-scatter.7.cloned.1.call-start = ((), (), s32[]{:S(2)}) async-start(), calls=%async_computation.9 | async-start | bytes 5918720
  179.6 18.8 %collective-permute-start.1 = (bf16[1088,2176]{1,0:T(8,128)(2,1)}, bf16[1088,2176]{1,0:T(8,128)(2,1)}, u32[]{:S(2)}, u32[]{:S(2)}) collective-permute-start(bf16[1088,2176]{1,0:T(8,128)(2,1)} %all-gather.2.cloned.1.call-done.down_ref), channel_id=1, source_target_pairs={{0,4},{4,0},{8,12},{12,8},{16,20},{20,16},{24,28},{28,24},{1,5},{5... | collective-permute-start | bytes 14204936 | tf_op jit(solution)/shard_map/ppermute | solution.py:1326
  184.6 5.1 collective-permute-start
  187.1 4.6 copy-start.9
  191.7 5.0 copy-start.18
  191.7 5.0 copy-start.19
  223.6 25.4 %collective-permute-start.2 = (bf16[1088,2176]{1,0:T(8,128)(2,1)}, bf16[1088,2176]{1,0:T(8,128)(2,1)S(1)}, u32[]{:S(2)}, u32[]{:S(2)}) collective-permute-start(bf16[1088,2176]{1,0:T(8,128)(2,1)} %get-tuple-element.79), channel_id=1, source_target_pairs={{0,4},{4,0},{8,12},{12,8},{16,20},{20,16},{24,28},{28,24},{1,5},{5... | collective-permute-start | bytes 14204936 | tf_op jit(solution)/shard_map/ppermute | solution.py:1326
  254.7 134.3 %reduce-scatter.9.cloned.1.call-start = ((), (), s32[]{:S(2)}) async-start(), calls=%async_computation.10 | async-start | bytes 5918720
  254.8 11.9 %collective-permute-start.4 = (bf16[1088,2176]{1,0:T(8,128)(2,1)}, bf16[1088,2176]{1,0:T(8,128)(2,1)S(1)}, u32[]{:S(2)}, u32[]{:S(2)}) collective-permute-start(bf16[1088,2176]{1,0:T(8,128)(2,1)} %get-tuple-element.88), channel_id=1, source_target_pairs={{0,4},{4,0},{8,12},{12,8},{16,20},{20,16},{24,28},{28,24},{1,5},{5... | collective-permute-start | bytes 14204936 | tf_op jit(solution)/shard_map/ppermute | solution.py:1326
  255.3 4.9 copy-start.3
  255.3 4.9 copy-start.5
  261.5 5.1 copy-start.16
  261.5 5.1 slice-start
  261.5 5.1 slice-start.1
  272.3 20.4 %all-to-all-start.2 = ((bf16[8,2,64,256]{3,2,1,0:T(8,128)(2,1)}), bf16[8,2,64,256]{3,2,1,0:T(8,128)(2,1)S(1)}, u32[]{:S(2)}, u32[]{:S(2)}) async-start(bf16[8,2,64,256]{3,2,1,0:T(8,128)(2,1)} %bitcast.139), calls=%async_computation.2 | async-start | bytes 1048576 | tf_op jit(solution)/shard_map/all_to_all | solution.py:1533
  292.8 25.4 %all-to-all-start.4 = ((bf16[8,3,64,256]{3,2,1,0:T(8,128)(2,1)}), bf16[8,3,64,256]{3,2,1,0:T(8,128)(2,1)}, u32[]{:S(2)}, u32[]{:S(2)}) async-start(bf16[8,3,64,256]{3,2,1,0:T(8,128)(2,1)} %pad_maximum_fusion.4), calls=%async_computation.4 | async-start | bytes 1572864 | tf_op jit(solution)/shard_map/all_to_all | solution.py:1534
  317.1 5.4 copy-start.17
  318.2 42.1 %all-to-all-start.3 = ((bf16[8,2,192,256]{3,2,1,0:T(8,128)(2,1)}), bf16[8,2,192,256]{3,2,1,0:T(8,128)(2,1)}, u32[]{:S(2)}, u32[]{:S(2)}) async-start(bf16[8,2,192,256]{3,2,1,0:T(8,128)(2,1)} %shard_map.209), calls=%async_computation.3 | async-start | bytes 3145728 | tf_op jit(solution)/shard_map/all_to_all | solution.py:1469
  327.8 37.7 %collective-permute-start.5 = (bf16[2,1088,384]{2,1,0:T(8,128)(2,1)}, bf16[2,1088,384]{2,1,0:T(8,128)(2,1)}, u32[]{:S(2)}, u32[]{:S(2)}) collective-permute-start(bf16[2,1088,384]{2,1,0:T(8,128)(2,1)} %bitcast.51), channel_id=1, source_target_pairs={{0,4},{4,0},{8,12},{12,8},{16,20},{20,16},{24,28},{28,24},{1,5},{5... | collective-permute-start | bytes 5013512 | tf_op jit(solution)/shard_map/ppermute | solution.py:1326
  329.0 10.4 %copy-start.27 = (f32[2,256]{1,0:T(2,128)}, f32[2,256]{1,0:T(2,128)S(1)}, u32[]{:S(2)}) copy-start(f32[2,256]{1,0:T(2,128)S(1)} %broadcast_multiply_fusion.2) | copy-start | bytes 6148
  329.3 184.4 %copy-start.32 = (f32[2,256]{1,0:T(2,128)}, f32[2,256]{1,0:T(2,128)S(1)}, u32[]{:S(2)}) copy-start(f32[2,256]{1,0:T(2,128)S(1)} %add_rsqrt_fusion) | copy-start | bytes 6148
  359.5 5.5 copy-start.30
  359.5 5.5 copy-start.31
  359.5 5.8 copy-start.22
  359.5 5.9 %copy-start.21 = (f32[1088]{0:T(1024)S(1)}, f32[1088]{0:T(1024)}, u32[]{:S(2)}) copy-start(f32[1088]{0:T(1024)} %get-tuple-element.113) | copy-start | bytes 13060
  359.5 6.0 %copy-start.13 = (bf16[1,2,4,272,384]{4,3,2,1,0:T(8,128)(2,1)S(1)}, bf16[1,2,4,272,384]{4,3,2,1,0:T(8,128)(2,1)}, u32[]{:S(2)}) copy-start(bf16[1,2,4,272,384]{4,3,2,1,0:T(8,128)(2,1)} %get-tuple-element.128) | copy-start | bytes 5013508
  360.3 149.7 %all-to-all-start.5 = ((bf16[8,2,192,256]{3,2,1,0:T(8,128)(2,1)}), bf16[8,2,192,256]{3,2,1,0:T(8,128)(2,1)}, u32[]{:S(2)}, u32[]{:S(2)}) async-start(bf16[8,2,192,256]{3,2,1,0:T(8,128)(2,1)} %shard_map.211), calls=%async_computation.5 | async-start | bytes 3145728 | tf_op jit(solution)/shard_map/all_to_all | solution.py:1469
  367.5 142.2 %collective-permute-start.3 = (bf16[1,192,256]{2,1,0:T(8,128)(2,1)S(1)}, bf16[1,192,256]{2,1,0:T(8,128)(2,1)S(1)}, u32[]{:S(2)}, u32[]{:S(2)}) collective-permute-start(bf16[1,192,256]{2,1,0:T(8,128)(2,1)S(1)} %dynamic-slice_bitcast_fusion), channel_id=1, source_target_pairs={{0,16},{4,20},{8,24},{12,28},{16,0},{20,4},{24,8},{28,12},{1,17},{... | collective-permute-start | bytes 294920 | tf_op jit(solution)/shard_map/ppermute | solution.py:1475
  524.1 40.0 %collective-permute-start.6 = (f32[12,272]{1,0:T(8,128)S(1)}, f32[12,272]{1,0:T(8,128)S(1)}, u32[]{:S(2)}, u32[]{:S(2)}) collective-permute-start(f32[12,272]{1,0:T(8,128)S(1)} %bitcast.195), channel_id=1, source_target_pairs={{0,1},{1,0},{2,3},{3,2},{4,5},{5,4},{6,7},{7,6},{8,9},{9,8},{10,11... | collective-permute-start | bytes 39176 | tf_op jit(solution)/shard_map/ppermute | solution.py:1621
  525.4 38.7 %collective-permute-start.7 = (f32[12,272]{1,0:T(8,128)S(1)}, f32[12,272]{1,0:T(8,128)S(1)}, u32[]{:S(2)}, u32[]{:S(2)}) collective-permute-start(f32[12,272]{1,0:T(8,128)S(1)} %bitcast.196), channel_id=1, source_target_pairs={{0,2},{1,3},{2,0},{3,1},{4,6},{5,7},{6,4},{7,5},{8,10},{9,11},{10,... | collective-permute-start | bytes 39176 | tf_op jit(solution)/shard_map/ppermute | solution.py:1621
  526.1 38.1 %collective-permute-start.8 = (f32[12,272]{1,0:T(8,128)S(1)}, f32[12,272]{1,0:T(8,128)S(1)}, u32[]{:S(2)}, u32[]{:S(2)}) collective-permute-start(f32[12,272]{1,0:T(8,128)S(1)} %bitcast.197), channel_id=1, source_target_pairs={{0,3},{1,2},{2,1},{3,0},{4,7},{5,6},{6,5},{7,4},{8,11},{9,10},{10,... | collective-permute-start | bytes 39176 | tf_op jit(solution)/shard_map/ppermute | solution.py:1621
  527.7 36.5 %copy-start.36 = (f32[2,256]{1,0:T(2,128)S(1)}, f32[2,256]{1,0:T(2,128)}, u32[]{:S(2)}) copy-start(f32[2,256]{1,0:T(2,128)} %get-tuple-element.110) | copy-start | bytes 6148
  527.7 37.7 %copy-start.35 = (f32[2,256]{1,0:T(2,128)S(1)}, f32[2,256]{1,0:T(2,128)}, u32[]{:S(2)}) copy-start(f32[2,256]{1,0:T(2,128)} %get-tuple-element.111) | copy-start | bytes 6148
  527.7 41.6 %copy-start.4 = (f32[2,1088,256]{2,1,0:T(8,128)S(1)}, f32[2,1088,256]{2,1,0:T(8,128)}, u32[]{:S(2)}) copy-start(f32[2,1088,256]{2,1,0:T(8,128)} %copy-done.2) | copy-start | bytes 6684676
  527.7 41.6 %copy-start.6 = (bf16[2,1088,256]{2,1,0:T(8,128)(2,1)S(1)}, bf16[2,1088,256]{2,1,0:T(8,128)(2,1)}, u32[]{:S(2)}) copy-start(bf16[2,1088,256]{2,1,0:T(8,128)(2,1)} %get-tuple-element.123.g_ref) | copy-start | bytes 3342340
  527.7 41.6 %copy-start.8 = (f32[2,1088,256]{2,1,0:T(8,128)S(1)}, f32[2,1088,256]{2,1,0:T(8,128)}, u32[]{:S(2)}) copy-start(f32[2,1088,256]{2,1,0:T(8,128)} %copy-done.7) | copy-start | bytes 6684676
  527.7 41.6 %copy-start.26 = (f32[2,256]{1,0:T(2,128)S(1)}, f32[2,256]{1,0:T(2,128)}, u32[]{:S(2)}) copy-start(f32[2,256]{1,0:T(2,128)} %copy-done.25) | copy-start | bytes 6148
  527.8 41.6 %copy-start.33 = (f32[2,256]{1,0:T(2,128)S(1)}, f32[2,256]{1,0:T(2,128)}, u32[]{:S(2)}) copy-start(f32[2,256]{1,0:T(2,128)} %copy-done.32) | copy-start | bytes 6148
  564.2 1.3 collective-permute-start.9
  565.4 3.8 collective-permute-start.10
  569.3 5.0 collective-permute-start.11
  569.3 4.9 copy-start.20
  569.3 4.9 copy-start.24
  569.3 4.9 copy-start.29
  (12 other events, 22.4 us)
Sparse Core Ops, SparseCore 0:
  120.7 58.8 all-gather.1
  254.8 59.3 reduce-scatter.6
  318.1 58.7 reduce-scatter.8
where the time goes:
time: 592 us; the launch traced here: 582 us
  Pallas kernels  408 us (69%)
  starting transfers between devices  38.7 us (7%)
  other arithmetic  37.3 us (6%)
  waiting for transfers between devices  33.8 us (6%)
  local copies, waits for them, and re-layouts  26.9 us (5%)
  matrix products  22.2 us (4%)
  between operations  15.2 us (3%)
    pallas_call x1, Pallas kernels, sum_grads(): pl.pallas_call(functools.partial(sum_kernel, ctx, fsdp, batches), in_spec...  121 us
    pallas_call x1, Pallas kernels, gather_first(): pl.pallas_call(functools.partial(gather_kernel, ctx, fsdp, regular), in_s...  109 us
    pallas_call x2, Pallas kernels, mlp(): pl.pallas_call(functools.partial(mlp_kernel, units), grid=(pl.cdiv(units,...  50.6 us
    pallas_call x3, Pallas kernels, attend_back(): pl.pallas_call(functools.partial(attend_back_kernel, block), grid_spec=pl...  46.6 us
    pallas_call x1, Pallas kernels, update(): pl.pallas_call(functools.partial(update_kernel, units, regular), grid=(ro...  36.4 us
    pallas_call x3, Pallas kernels, attend(): pl.pallas_call(functools.partial(attend_kernel, block), grid_spec=pltpu.P...  31.6 us
    all_to_all x4, starting transfers between devices, to_rows(): got = lax.all_to_all(array, 'ctx', 0, 0)  19.2 us
    all_to_all x1, waiting for transfers between devices, body(): first_pairs = lax.all_to_all(to_send(grad_att[0, :-1]), 'ctx', 0, 0)  13.5 us
  transfers between devices with their start and end apart: 21, of which 9 were waited for; matrix products, arithmetic and copies ran while one was open for 10% of the time, Pallas kernels for 47%

commit v1 on v0

--- a/solution.py
+++ b/solution.py
@@ -768,15 +768,17 @@
         if unit == 0:
             done = max(time, block_time * (chips - 1))
     at(done + 0.3, ready)
+    time = done + 0.9
     for h in range(slots):
         for s in range(-1, chips - 1):
-            arrived = block_time * (h * (chips - 1) + s + 1) + 0.1
-            late = max(arrived, done + 0.31 + 0.2 * (s + 1) + 0.01 * h)
+            arrived = block_time * (h * (chips - 1) + s + 1)
+            time = max(time, arrived + 0.1)
             if s < 0:
-                at(late, project_own, h)
+                at(time, project_own, h)
             else:
-                at(late, project_step, h, s)
-        at(max(arrived, done + 0.31 + 0.2 * chips) + 0.02, lambda h: out_copy(h).start(), h)
+                at(time, project_step, h, s)
+            time += 0.2 if s < 0 else 0.4
+        at(time, lambda h: out_copy(h).start(), h)
 
     fetch(0).start()
     fetch(1).start()
@@ -1518,19 +1520,20 @@
     output = (mid + (y_mine + y_other + vec[7])).astype(BF16).transpose(2, 0, 1)
 
     up_swapped, down_swapped = swap_cores(dup_other, ctx), swap_cores(ddown_other, ctx)
+
     up_total = add_low(dup_mine, up_swapped)
     up_part = scatter_fsdp(up_total)
     ga_mine = after(ga_mine, up_total)
-
     grad_mid, gain_two, shift_two = norm_back(ga_mine + ga_other, unit_two, inverse_two, vec[5])
     grad_mid = g + grad_mid
     grad_attn = grad_mid.astype(BF16)
     grad_att = jnp.einsum("de,set->sdt", out_w, grad_attn, preferred_element_type=F32).astype(BF16)
-    down_part = scatter_fsdp(add_low(after(ddown_mine, grad_att), down_swapped))
-    grad_attn_later = after(grad_attn, grad_att)
     grad_att = grad_att.reshape(slots, HEADS, dim, tok)
+    first_send = to_send(grad_att[0, :-1])
+    grad_attn_later = after(grad_attn, first_send)
     last = jnp.repeat(grad_att[:, -1], ctx // slots, axis=0)[:, None]
-    first_pairs = lax.all_to_all(to_send(grad_att[0, :-1]), "ctx", 0, 0)
+    first_pairs = lax.all_to_all(first_send, "ctx", 0, 0)
+    down_part = scatter_fsdp(add_low(after(ddown_mine, first_pairs), down_swapped))
     other_pairs = lax.all_to_all(
         after(jnp.concatenate([to_send(grad_att[1, :-1]), last], axis=1), first_pairs), "ctx", 0, 0
     )

time: 592 us -> 577 us (0.975)
  blocking collectives: 0 us -> 20.2 us
  waiting for transfers between devices: 33.8 us -> 20.6 us
  Pallas kernels: 408 us -> 395 us
  starting transfers between devices: 38.7 us -> 32.2 us
    all_to_all x0 -> x1, blocking collectives: none -> 20.2 us  [body(): first_pairs = lax.all_to_all(first_send, 'ctx', 0, 0)]
    all_to_all x1 -> x0, waiting for transfers between devices: 13.5 us -> none  [body(): first_pairs = lax.all_to_all(to_send(grad_att[0, :-1]), 'ctx', 0, 0)]
    pallas_call x1, Pallas kernels: 109 us -> 96.2 us  [gather_first(): pl.pallas_call(functools.partial(gather_kernel, ctx, fsdp, regular), in_s...]
  transfers between devices with their start and end apart: 21 -> 20, of which waited for: 9 -> 8; matrix products, arithmetic and copies ran while one was open for 10% -> 10% of each run, Pallas kernels for 47% -> 48%
where the time goes in v1:
time: 577 us; the launch traced here: 567 us
  Pallas kernels  395 us (68%)
  other arithmetic  37.3 us (6%)
  starting transfers between devices  32.2 us (6%)
  local copies, waits for them, and re-layouts  24.8 us (4%)
  matrix products  21.2 us (4%)
  waiting for transfers between devices  20.6 us (4%)
  blocking collectives  20.2 us (4%)
  between operations  15.2 us (3%)
    pallas_call x1, Pallas kernels, sum_grads(): pl.pallas_call(functools.partial(sum_kernel, ctx, fsdp, batches), in_spec...  121 us
    pallas_call x1, Pallas kernels, gather_first(): pl.pallas_call(functools.partial(gather_kernel, ctx, fsdp, regular), in_s...  96.2 us
    pallas_call x2, Pallas kernels, mlp(): pl.pallas_call(functools.partial(mlp_kernel, units), grid=(pl.cdiv(units,...  50.6 us
    pallas_call x3, Pallas kernels, attend_back(): pl.pallas_call(functools.partial(attend_back_kernel, block), grid_spec=pl...  46.4 us
    pallas_call x1, Pallas kernels, update(): pl.pallas_call(functools.partial(update_kernel, units, regular), grid=(ro...  36.4 us
    pallas_call x3, Pallas kernels, attend(): pl.pallas_call(functools.partial(attend_kernel, block), grid_spec=pltpu.P...  31.7 us
    all_to_all x1, blocking collectives, body(): first_pairs = lax.all_to_all(first_send, 'ctx', 0, 0)  20.2 us
    all_to_all x4, starting transfers between devices, to_rows(): got = lax.all_to_all(array, 'ctx', 0, 0)  17.8 us
  transfers between devices with their start and end apart: 20, of which 8 were waited for; matrix products, arithmetic and copies ran while one was open for 10% of the time, Pallas kernels for 48%

profile of v1, /device:TPU:0, one launch (start us, length us, event | category | flops | bytes accessed | tf_op | source)
XLA Modules:
  0.0 566.7 jit_solution(12952409840761170220)
XLA Ops:
  8.1 2.8 fusion.17
  11.6 96.2 %shard_map.203 = (bf16[2,8,1088,256]{3,2,1,0:T(8,128)(2,1)}, bf16[2,576,2048]{2,1,0:T(8,128)(2,1)}, bf16[4,272,4352]{2,1,0:T(8,128)(2,1)}, bf16[4,272,2176]{2,1,...) custom-call(bf16[2,1088,256]{2,1,0:T(8,128)(2,1)} %bitcast.157, f32[272,8704]{1,0:T(8,128)} %refs_0_.1, ...), custom_call_target="tpu_custom_call" | custom-call | flops 1000 | bytes 1000 | tf_op jit(solution)/shard_map/pallas_call | solution.py:835
  109.1 12.5 %shard_map.204 = (f32[2,64,2048]{2,1,0:T(8,128)S(1)}, bf16[8,2,64,256]{3,2,1,0:T(8,128)(2,1)}, f32[2,1,2048]{2,1,0:T(1,128)S(1)}) custom-call(s32[2]{0:T(128)S(1)} %reshape.210.lens_ref, bf16[2,3,3,64,2048]{4,3,2,1,0:T(8,128)(2,1)} %bitcast.144, bf16[2,3,3,64,2048]{4,3,2,1,0:T(8,128)(2,1)} %bitcast.145, bf16[2,3,3,64,2048]{4,3,2,1,0:T(8,128)(2,1)} %bitcast.146), custom_call_target="tpu_custom_call" | custom-call | flops 1000 | bytes 1000 | tf_op jit(solution)/shard_map/pallas_call | solution.py:114
  122.6 4.8 all-to-all-start
  128.0 12.1 %shard_map.205 = (f32[2,64,2048]{2,1,0:T(8,128)S(1)}, bf16[8,2,64,256]{3,2,1,0:T(8,128)(2,1)}, f32[2,1,2048]{2,1,0:T(1,128)S(1)}) custom-call(s32[2]{0:T(128)S(1)} %reshape.213.lens_ref, bf16[2,3,3,64,2048]{4,3,2,1,0:T(8,128)(2,1)} %bitcast.147, bf16[2,3,3,64,2048]{4,3,2,1,0:T(8,128)(2,1)} %bitcast.148, bf16[2,3,3,64,2048]{4,3,2,1,0:T(8,128)(2,1)} %bitcast.149), custom_call_target="tpu_custom_call" | custom-call | flops 1000 | bytes 1000 | tf_op jit(solution)/shard_map/pallas_call | solution.py:114
  140.2 2.6 all-to-all-done
  142.7 4.1 all-to-all-start.1
  146.9 1.5 slice_select_fusion.q_ref.k_ref.v_ref
  148.4 7.1 %shard_map.206 = (f32[1,64,2048]{2,1,0:T(8,128)S(1)}, bf16[8,1,64,256]{3,2,1,0:T(8,128)(2,1)S(1)}, f32[1,1,2048]{2,1,0:T(1,128)S(1)}) custom-call(s32[1]{0:T(128)} %get-tuple-element.64.lens_ref, bf16[1,3,1,64,2048]{4,3,2,1,0:T(8,128)(2,1)S(1)} %slice_select_fusion.q_ref.k_ref.v_ref, bf16[1,3,1,64,2048]{4,3,2,1,0:T(8,128)(2,1)S(1)} %slice_select_fusion.q_ref.k_ref.v_ref, ...), custom_call_target="tpu_custom_call" | custom-call | flops 1000 | bytes 1000 | tf_op jit(solution)/shard_map/pallas_call | solution.py:114
  155.6 6.7 %all-to-all-done.1 = bf16[8,2,64,256]{3,2,1,0:T(8,128)(2,1)} async-done(((bf16[8,2,64,256]{3,2,1,0:T(8,128)(2,1)}), bf16[8,2,64,256]{3,2,1,0:T(8,128)(2,1)}, u32[]{:S(2)}, u32[]{:S(2)}) %all-to-all-start.1) | async-done | bytes 524320 | tf_op jit(solution)/shard_map/all_to_all | solution.py:1471
  162.2 1.9 copy.66
  164.1 1.4 all-gather.2.cloned.1.call-done.down_ref
  166.9 2.5 convert_reduce_fusion.2
  170.6 2.4 collective-permute-start
  173.1 2.7 collective-permute-done
  177.7 4.9 fusion.40
  182.9 1.4 add_convert_fusion.3.a_ref
  184.4 25.2 %shard_map.208 = (f32[2,1088,256]{2,1,0:T(8,128)}, f32[2,1088,256]{2,1,0:T(8,128)}, bf16[1088,2176]{1,0:T(8,128)(2,1)}, bf16[1088,2176]{1,0:T(8,128)(2,1)}, f32[1,2176]{1,0:T(1,128)}) custom-call(bf16[2,1088,256]{2,1,0:T(8,128)(2,1)} %add_convert_fusion.3.a_ref, bf16[2,1088,256]{2,1,0:T(8,128)(2,1)} %get-tuple-element.123.g_ref, ...), custom_call_target="tpu_custom_call" | custom-call | flops 1000 | bytes 1000 | tf_op jit(solution)/shard_map/pallas_call | solution.py:369
  209.6 25.4 %shard_map.207 = (f32[2,1088,256]{2,1,0:T(8,128)}, f32[2,1088,256]{2,1,0:T(8,128)}, bf16[1088,2176]{1,0:T(8,128)(2,1)}, bf16[1088,2176]{1,0:T(8,128)(2,1)}, f32[1,2176]{1,0:T(1,128)}) custom-call(bf16[2,1088,256]{2,1,0:T(8,128)(2,1)} %add_convert_fusion.3.a_ref, bf16[2,1088,256]{2,1,0:T(8,128)(2,1)} %get-tuple-element.123.g_ref, ...), custom_call_target="tpu_custom_call" | custom-call | flops 1000 | bytes 1000 | tf_op jit(solution)/shard_map/pallas_call | solution.py:369
  235.0 5.7 %add_convert_fusion.1 = bf16[1088,2176]{1,0:T(8,128)(2,1)} fusion(bf16[1088,2176]{1,0:T(8,128)(2,1)S(1)} %collective-permute-done.2, bf16[1088,2176]{1,0:T(8,128)(2,1)} %get-tuple-element.78), kind=kLoop, calls=%fused_computation.1 | loop fusion | flops 9469952 | bytes 14204928 | tf_op jit(solution)/shard_map/convert_element_type | solution.py:902
  241.3 4.9 multiply_reduce_fusion
  247.5 4.1 convolution_convert_fusion
  251.8 20.2 %all_to_all.30.grad_ref = bf16[8,2,64,256]{3,2,1,0:T(8,128)(2,1)S(1)} all-to-all(bf16[8,2,64,256]{3,2,1,0:T(8,128)(2,1)S(1)} %bitcast.181), channel_id=1, replica_groups=mesh['ctx'=8,'fsdp'=4] {'ctx'}, dimensions={0} | all-to-all | bytes 1048576 | tf_op jit(solution)/shard_map/all_to_all | solution.py:1535
  272.0 3.5 add_convert_fusion
  277.4 4.4 all-to-all-start.4
  281.8 1.3 copy-done.1
  283.1 18.6 %shard_map.209 = bf16[8,2,192,256]{3,2,1,0:T(8,128)(2,1)} custom-call(s32[2]{0:T(128)S(1)} %reshape.210.lens_ref, bf16[2,3,3,64,2048]{4,3,2,1,0:T(8,128)(2,1)} %bitcast.151, bf16[2,3,3,64,2048]{4,3,2,1,0:T(8,128)(2,1)} %bitcast.152, bf16[2,3,3,64,2048]{4,3,2,1,0:T(8,128)(2,1)} %bitcast.153, f32[2,64,2048]{2,1,0:T(8,128)S(1)} %copy-done.1, ...), custom_call_target="tpu_custom_call" | custom-call | flops 1000 | bytes 1000 | tf_op jit(solution)/shard_map/pallas_call | solution.py:220
  302.8 4.3 all-to-all-start.3
  307.1 3.2 bitcast_convert_fusion
  310.3 2.1 constant_dynamic-slice_fusion.4
  314.9 9.2 %shard_map.210 = bf16[8,1,192,256]{3,2,1,0:T(8,128)(2,1)S(1)} custom-call(s32[1]{0:T(128)} %get-tuple-element.64.lens_ref, bf16[1,3,1,64,2048]{4,3,2,1,0:T(8,128)(2,1)S(1)} %slice_select_fusion.q_ref.k_ref.v_ref, bf16[1,3,1,64,2048]{4,3,2,1,0:T(8,128)(2,1)S(1)} %slice_select_fusion.q_ref.k_ref.v_ref, ...), custom_call_target="tpu_custom_call" | custom-call | flops 1000 | bytes 1000 | tf_op jit(solution)/shard_map/pallas_call | solution.py:220
  325.3 18.6 %shard_map.211 = bf16[8,2,192,256]{3,2,1,0:T(8,128)(2,1)} custom-call(s32[2]{0:T(128)S(1)} %reshape.213.lens_ref, bf16[2,3,3,64,2048]{4,3,2,1,0:T(8,128)(2,1)} %bitcast.154, bf16[2,3,3,64,2048]{4,3,2,1,0:T(8,128)(2,1)} %bitcast.155, bf16[2,3,3,64,2048]{4,3,2,1,0:T(8,128)(2,1)} %bitcast.156, f32[2,64,2048]{2,1,0:T(8,128)S(1)} %get-tuple-element.63.o_ref, ...), custom_call_target="tpu_custom_call" | custom-call | flops 1000 | bytes 1000 | tf_op jit(solution)/shard_map/pallas_call | solution.py:220
  344.9 4.6 all-to-all-start.5
  350.0 1.9 fusion.1
  352.0 2.9 collective-permute-start.3
  355.0 1.5 copy.75
  356.5 13.0 %shard_map.212 = f32[1088,576]{1,0:T(8,128)} custom-call(s32[1]{0:T(128)} %bitcast.37.late_ref, bf16[2,8,1088,256]{3,2,1,0:T(8,128)(2,1)} %get-tuple-element.89.first_ref.second_ref, bf16[2,8,1088,256]{3,2,1,0:T(8,128)(2,1)} %get-tuple-element.89.first_ref.second_ref, bf16[8,384,256]{2,1,0:T(8,128)(2,1)} %bitcast.38.first_grad_ref, ...), custom_call_target="tpu_custom_call" | custom-call | flops 1000 | bytes 1000 | tf_op jit(solution)/shard_map/pallas_call | solution.py:283
  369.5 1.9 convert_element_type.117
  371.7 1.8 pad_maximum_fusion.1.refs_2_
  373.5 120.9 %shard_map.213 = (bf16[2,272,2560]{2,1,0:T(8,128)(2,1)}, bf16[2,272,2560]{2,1,0:T(8,128)(2,1)}, bf16[8,272,384]{2,1,0:T(8,128)(2,1)}, bf16[2,272,256]{2,1,0:T(8,128)(2,1)}) custom-call(bf16[272,2176]{1,0:T(8,128)(2,1)} %reduce-scatter.7.cloned.1.call-done.refs_0_, bf16[272,2176]{1,0:T(8,128)(2,1)} %reduce-scatter.9.cloned.1.call-done.refs_1_, ...), custom_call_target="tpu_custom_call" | custom-call | flops 1000 | bytes 1000 | tf_op jit(solution)/shard_map/pallas_call | solution.py:1294
  494.8 2.1 copy.79
  499.1 9.0 %fusion.13 = (f32[1088]{0:T(1024)S(1)}, f32[2,256]{1,0:T(2,128)}, f32[2,256]{1,0:T(2,128)}, f32[2,256,1088]{1,2,0:T(8,128)S(1)}) fusion(f32[2,256]{1,0:T(2,128)S(1)} %add_rsqrt_fusion, f32[2,256]{1,0:T(2,128)S(1)} %copy-done.29, bf16[256,2,1088]{0,2,1:T(8,128)(2,1)S(1)} %copy-done.11, f32[1088]{0:T(1024)S(1)} %get-tuple-element.114, ...), kind=kOutput, calls=%fused_computation.30 | convolution fusion | flops 3648157696 | bytes 13943296 | tf_op jit(solution)/shard_map/de,set->sdt/dot_general | solution.py:1598
  508.9 1.3 collective-permute-start.6
  511.1 1.3 collective-permute-start.8
  512.5 36.4 %shard_map.214 = (f32[272,8704]{1,0:T(8,128)}, f32[272,8704]{1,0:T(8,128)}, f32[272,8704]{1,0:T(8,128)}, f32[272,4352]{1,0:T(8,128)}, f32[272,4352]{1,0:T(8,128)}, /*index=5*/f32[272,4352]{1,0:T(8,128)}) custom-call(f32[272,8704]{1,0:T(8,128)} %refs_0_.1, bf16[272,8704]{1,0:T(8,128)(2,1)} %refs_1_.1, f32[272,8704]{1,0:T(8,128)} %refs_2_.1, ...), custom_call_target="tpu_custom_call" | custom-call | flops 1000 | bytes 1000 | tf_op jit(solution)/shard_map/pallas_call | solution.py:1413
  549.0 1.2 collective-permute-done.9
  550.2 3.8 collective-permute-done.10
  554.1 4.9 fusion.19
  (186 shorter events, 24.8 us)
Async XLA Ops:
  7.2 158.4 %all-gather.2.cloned.1.call-start = ((), (), s32[]{:S(2)}) async-start(), calls=%async_computation.8 | async-start | bytes 5918720 | tf_op jit(solution)/shard_map/all_gather | solution.py:1462
  11.6 96.2 %copy-start.35 = (s32[2]{0:T(128)S(1)}, s32[2]{0:T(128)}, u32[]{:S(2)}) copy-start(s32[2]{0:T(128)} %param.14) | copy-start | bytes 28
  122.6 20.1 %all-to-all-start = ((bf16[8,2,64,256]{3,2,1,0:T(8,128)(2,1)}), bf16[8,2,64,256]{3,2,1,0:T(8,128)(2,1)S(1)}, u32[]{:S(2)}, u32[]{:S(2)}) async-start(bf16[8,2,64,256]{3,2,1,0:T(8,128)(2,1)} %get-tuple-element.60), calls=%async_computation | async-start | bytes 1048576 | tf_op jit(solution)/shard_map/all_to_all | solution.py:1471
  142.7 19.5 %all-to-all-start.1 = ((bf16[8,2,64,256]{3,2,1,0:T(8,128)(2,1)}), bf16[8,2,64,256]{3,2,1,0:T(8,128)(2,1)}, u32[]{:S(2)}, u32[]{:S(2)}) async-start(bf16[8,2,64,256]{3,2,1,0:T(8,128)(2,1)} %get-tuple-element.66), calls=%async_computation.1 | async-start | bytes 1048576 | tf_op jit(solution)/shard_map/all_to_all | solution.py:1471
  146.9 178.4 %reduce-scatter.7.cloned.1.call-start = ((), (), s32[]{:S(2)}) async-start(), calls=%async_computation.9 | async-start | bytes 5918720
  165.5 18.8 %collective-permute-start.1 = (bf16[1088,2176]{1,0:T(8,128)(2,1)}, bf16[1088,2176]{1,0:T(8,128)(2,1)}, u32[]{:S(2)}, u32[]{:S(2)}) collective-permute-start(bf16[1088,2176]{1,0:T(8,128)(2,1)} %all-gather.2.cloned.1.call-done.down_ref), channel_id=1, source_target_pairs={{0,4},{4,0},{8,12},{12,8},{16,20},{20,16},{24,28},{28,24},{1,5},{5... | collective-permute-start | bytes 14204936 | tf_op jit(solution)/shard_map/ppermute | solution.py:1328
  170.6 5.1 collective-permute-start
  173.0 4.6 copy-start.9
  177.7 5.0 copy-start.19
  177.7 5.0 copy-start.20
  209.6 25.4 %collective-permute-start.2 = (bf16[1088,2176]{1,0:T(8,128)(2,1)}, bf16[1088,2176]{1,0:T(8,128)(2,1)S(1)}, u32[]{:S(2)}, u32[]{:S(2)}) collective-permute-start(bf16[1088,2176]{1,0:T(8,128)(2,1)} %get-tuple-element.79), channel_id=1, source_target_pairs={{0,4},{4,0},{8,12},{12,8},{16,20},{20,16},{24,28},{28,24},{1,5},{5... | collective-permute-start | bytes 14204936 | tf_op jit(solution)/shard_map/ppermute | solution.py:1328
  240.7 132.8 %reduce-scatter.9.cloned.1.call-start = ((), (), s32[]{:S(2)}) async-start(), calls=%async_computation.10 | async-start | bytes 5918720
  240.7 31.2 %collective-permute-start.4 = (bf16[1088,2176]{1,0:T(8,128)(2,1)}, bf16[1088,2176]{1,0:T(8,128)(2,1)S(1)}, u32[]{:S(2)}, u32[]{:S(2)}) collective-permute-start(bf16[1088,2176]{1,0:T(8,128)(2,1)} %get-tuple-element.88), channel_id=1, source_target_pairs={{0,4},{4,0},{8,12},{12,8},{16,20},{20,16},{24,28},{28,24},{1,5},{5... | collective-permute-start | bytes 14204936 | tf_op jit(solution)/shard_map/ppermute | solution.py:1328
  241.3 4.9 copy-start.3
  241.3 4.9 copy-start.5
  247.5 24.5 %slice-start = ((s8[4734976]{0:T(1024)(128)(4,1)}), s8[4194304]{0:T(1024)(128)(4,1)S(1)}, s32[]{:S(2)}) async-start(s8[4734976]{0:T(1024)(128)(4,1)} %bitcast.169), calls=%async_computation.11 | async-start | bytes 8388608
  247.5 24.5 %slice-start.1 = ((s8[4734976]{0:T(1024)(128)(4,1)}), s8[540672]{0:T(1024)(128)(4,1)S(1)}, s32[]{:S(2)}) async-start(s8[4734976]{0:T(1024)(128)(4,1)} %bitcast.169), calls=%async_computation.12 | async-start | bytes 1081344
  251.6 20.3 %copy-start.18 = (bf16[2,256,1088]{1,2,0:T(8,128)(2,1)}, bf16[2,256,1088]{1,2,0:T(8,128)(2,1)S(1)}, u32[]{:S(2)}) copy-start(bf16[2,256,1088]{1,2,0:T(8,128)(2,1)S(1)} %convolution_convert_fusion) | copy-start | bytes 3342340
  277.4 25.4 %all-to-all-start.4 = ((bf16[8,3,64,256]{3,2,1,0:T(8,128)(2,1)}), bf16[8,3,64,256]{3,2,1,0:T(8,128)(2,1)}, u32[]{:S(2)}, u32[]{:S(2)}) async-start(bf16[8,3,64,256]{3,2,1,0:T(8,128)(2,1)} %pad_maximum_fusion.4), calls=%async_computation.4 | async-start | bytes 1572864 | tf_op jit(solution)/shard_map/all_to_all | solution.py:1537
  301.7 5.4 copy-start.17
  302.8 42.2 %all-to-all-start.3 = ((bf16[8,2,192,256]{3,2,1,0:T(8,128)(2,1)}), bf16[8,2,192,256]{3,2,1,0:T(8,128)(2,1)}, u32[]{:S(2)}, u32[]{:S(2)}) async-start(bf16[8,2,192,256]{3,2,1,0:T(8,128)(2,1)} %shard_map.209), calls=%async_computation.3 | async-start | bytes 3145728 | tf_op jit(solution)/shard_map/all_to_all | solution.py:1471
  312.4 37.6 %collective-permute-start.5 = (bf16[2,1088,384]{2,1,0:T(8,128)(2,1)}, bf16[2,1088,384]{2,1,0:T(8,128)(2,1)}, u32[]{:S(2)}, u32[]{:S(2)}) collective-permute-start(bf16[2,1088,384]{2,1,0:T(8,128)(2,1)} %bitcast.51), channel_id=1, source_target_pairs={{0,4},{4,0},{8,12},{12,8},{16,20},{20,16},{24,28},{28,24},{1,5},{5... | collective-permute-start | bytes 5013512 | tf_op jit(solution)/shard_map/ppermute | solution.py:1328
  313.6 10.5 %copy-start.28 = (f32[2,256]{1,0:T(2,128)}, f32[2,256]{1,0:T(2,128)S(1)}, u32[]{:S(2)}) copy-start(f32[2,256]{1,0:T(2,128)S(1)} %broadcast_multiply_fusion.2) | copy-start | bytes 6148
  314.0 184.5 %copy-start.33 = (f32[2,256]{1,0:T(2,128)}, f32[2,256]{1,0:T(2,128)S(1)}, u32[]{:S(2)}) copy-start(f32[2,256]{1,0:T(2,128)S(1)} %add_rsqrt_fusion) | copy-start | bytes 6148
  343.8 5.7 copy-start.31
  343.8 5.7 %copy-start.32 = (f32[1,2176]{1,0:T(1,128)S(1)}, f32[1,2176]{1,0:T(1,128)}, u32[]{:S(2)}) copy-start(f32[1,2176]{1,0:T(1,128)} %get-tuple-element.105) | copy-start | bytes 26116
  343.8 5.9 %copy-start.23 = (f32[1088]{0:T(1024)S(1)}, f32[1088]{0:T(1024)}, u32[]{:S(2)}) copy-start(f32[1088]{0:T(1024)} %get-tuple-element.107) | copy-start | bytes 13060
  343.8 6.0 %copy-start.22 = (f32[1088]{0:T(1024)S(1)}, f32[1088]{0:T(1024)}, u32[]{:S(2)}) copy-start(f32[1088]{0:T(1024)} %get-tuple-element.113) | copy-start | bytes 13060
  343.9 6.1 %copy-start.13 = (bf16[1,2,4,272,384]{4,3,2,1,0:T(8,128)(2,1)S(1)}, bf16[1,2,4,272,384]{4,3,2,1,0:T(8,128)(2,1)}, u32[]{:S(2)}) copy-start(bf16[1,2,4,272,384]{4,3,2,1,0:T(8,128)(2,1)} %get-tuple-element.128) | copy-start | bytes 5013508
  344.9 149.8 %all-to-all-start.5 = ((bf16[8,2,192,256]{3,2,1,0:T(8,128)(2,1)}), bf16[8,2,192,256]{3,2,1,0:T(8,128)(2,1)}, u32[]{:S(2)}, u32[]{:S(2)}) async-start(bf16[8,2,192,256]{3,2,1,0:T(8,128)(2,1)} %shard_map.211), calls=%async_computation.5 | async-start | bytes 3145728 | tf_op jit(solution)/shard_map/all_to_all | solution.py:1471
  352.0 142.4 %collective-permute-start.3 = (bf16[1,192,256]{2,1,0:T(8,128)(2,1)S(1)}, bf16[1,192,256]{2,1,0:T(8,128)(2,1)S(1)}, u32[]{:S(2)}, u32[]{:S(2)}) collective-permute-start(bf16[1,192,256]{2,1,0:T(8,128)(2,1)S(1)} %dynamic-slice_bitcast_fusion), channel_id=1, source_target_pairs={{0,16},{4,20},{8,24},{12,28},{16,0},{20,4},{24,8},{28,12},{1,17},{... | collective-permute-start | bytes 294920 | tf_op jit(solution)/shard_map/ppermute | solution.py:1477
  508.1 4.4 copy-start.12
  508.9 40.0 %collective-permute-start.6 = (f32[12,272]{1,0:T(8,128)S(1)}, f32[12,272]{1,0:T(8,128)S(1)}, u32[]{:S(2)}, u32[]{:S(2)}) collective-permute-start(f32[12,272]{1,0:T(8,128)S(1)} %bitcast.196), channel_id=1, source_target_pairs={{0,1},{1,0},{2,3},{3,2},{4,5},{5,4},{6,7},{7,6},{8,9},{9,8},{10,11... | collective-permute-start | bytes 39176 | tf_op jit(solution)/shard_map/ppermute | solution.py:1624
  510.2 38.7 %collective-permute-start.7 = (f32[12,272]{1,0:T(8,128)S(1)}, f32[12,272]{1,0:T(8,128)S(1)}, u32[]{:S(2)}, u32[]{:S(2)}) collective-permute-start(f32[12,272]{1,0:T(8,128)S(1)} %bitcast.197), channel_id=1, source_target_pairs={{0,2},{1,3},{2,0},{3,1},{4,6},{5,7},{6,4},{7,5},{8,10},{9,11},{10,... | collective-permute-start | bytes 39176 | tf_op jit(solution)/shard_map/ppermute | solution.py:1624
  511.1 37.8 %collective-permute-start.8 = (f32[12,272]{1,0:T(8,128)S(1)}, f32[12,272]{1,0:T(8,128)S(1)}, u32[]{:S(2)}, u32[]{:S(2)}) collective-permute-start(f32[12,272]{1,0:T(8,128)S(1)} %bitcast.198), channel_id=1, source_target_pairs={{0,3},{1,2},{2,1},{3,0},{4,7},{5,6},{6,5},{7,4},{8,11},{9,10},{10,... | collective-permute-start | bytes 39176 | tf_op jit(solution)/shard_map/ppermute | solution.py:1624
  512.5 36.5 %copy-start.37 = (f32[2,256]{1,0:T(2,128)S(1)}, f32[2,256]{1,0:T(2,128)}, u32[]{:S(2)}) copy-start(f32[2,256]{1,0:T(2,128)} %get-tuple-element.110) | copy-start | bytes 6148
  512.5 37.7 %copy-start.36 = (f32[2,256]{1,0:T(2,128)S(1)}, f32[2,256]{1,0:T(2,128)}, u32[]{:S(2)}) copy-start(f32[2,256]{1,0:T(2,128)} %get-tuple-element.111) | copy-start | bytes 6148
  512.5 41.6 %copy-start.4 = (f32[2,1088,256]{2,1,0:T(8,128)S(1)}, f32[2,1088,256]{2,1,0:T(8,128)}, u32[]{:S(2)}) copy-start(f32[2,1088,256]{2,1,0:T(8,128)} %copy-done.2) | copy-start | bytes 6684676
  512.5 41.6 %copy-start.6 = (bf16[2,1088,256]{2,1,0:T(8,128)(2,1)S(1)}, bf16[2,1088,256]{2,1,0:T(8,128)(2,1)}, u32[]{:S(2)}) copy-start(bf16[2,1088,256]{2,1,0:T(8,128)(2,1)} %get-tuple-element.123.g_ref) | copy-start | bytes 3342340
  512.5 41.6 %copy-start.8 = (f32[2,1088,256]{2,1,0:T(8,128)S(1)}, f32[2,1088,256]{2,1,0:T(8,128)}, u32[]{:S(2)}) copy-start(f32[2,1088,256]{2,1,0:T(8,128)} %copy-done.7) | copy-start | bytes 6684676
  512.5 41.6 %copy-start.27 = (f32[2,256]{1,0:T(2,128)S(1)}, f32[2,256]{1,0:T(2,128)}, u32[]{:S(2)}) copy-start(f32[2,256]{1,0:T(2,128)} %copy-done.26) | copy-start | bytes 6148
  512.5 41.6 %copy-start.34 = (f32[2,256]{1,0:T(2,128)S(1)}, f32[2,256]{1,0:T(2,128)}, u32[]{:S(2)}) copy-start(f32[2,256]{1,0:T(2,128)} %copy-done.33) | copy-start | bytes 6148
  548.9 1.3 collective-permute-start.9
  550.2 3.8 collective-permute-start.10
  554.0 5.0 collective-permute-start.11
  554.1 4.9 copy-start.21
  554.1 4.9 copy-start.25
  554.1 4.9 copy-start.30
  (12 other events, 22.0 us)
Sparse Core Ops, SparseCore 0:
  107.9 57.5 all-gather.1
  240.8 59.3 reduce-scatter.6
  304.1 58.6 reduce-scatter.8

commit v2 on v1

--- a/solution.py
+++ b/solution.py
@@ -1005,11 +1005,13 @@
 def sum_kernel(ctx, fsdp, batches, *refs):
     levels, chips = bits_of(fsdp), ctx // 2
     pieces = refs[0:2]
-    own_ref, mine_out, other_out, own_out, last_out = refs[2:7]
-    rest = list(refs[7:])
-    own_kept, own_low, beside = rest.pop(0), rest.pop(0), rest.pop(0)
-    own_sent = [rest.pop(0) for _ in range(levels)]
-    own_got = [rest.pop(0) for _ in range(levels)]
+    group_refs = refs[2:4]
+    mine_out, other_out, own_out, last_out = refs[4:8]
+    rest = list(refs[8:])
+    own_kept = [rest.pop(0) for _ in range(2)]
+    own_low, beside = rest.pop(0), rest.pop(0)
+    own_sent = [[rest.pop(0) for _ in range(levels)] for _ in range(2)]
+    own_got = [[rest.pop(0) for _ in range(levels)] for _ in range(2)]
     z_sent, z_got = rest.pop(0), rest.pop(0)
     op_send, op_recv, zs_send, zs_recv, zg_send, zg_recv = (rest.pop(0) for _ in range(6))
     zc_send, zc_recv, og_send, og_recv, oc_send, oc_recv, far_send, far_recv, local = (
@@ -1079,21 +1081,25 @@
     def across(step, q):
         return (c, other_index(f, 1 << order(q)[step]))
 
-    def own_copy(step):
+    def own_copy(g, step):
         return remote_copy(
-            own_sent[step], own_got[step], op_send.at[step], op_recv.at[step], across(step, 0)
+            own_sent[g][step],
+            own_got[g][step],
+            op_send.at[g, step],
+            op_recv.at[g, step],
+            across(step, g),
         )
 
-    def own_begin():
+    def own_begin(g):
         for free in range(fsdp // 2):
-            there, here = place_of(0, True, free), place_of(0, False, free)
+            there, here = place_of(g, True, free), place_of(g, False, free)
 
             def work(at, free=free, there=there, here=here):
-                own_sent[0][free, at, :] = own_ref[there, at, :]
-                own_kept[free, at, :] = own_ref[here, at, :].astype(F32)
+                own_sent[g][0][free, at, :] = group_refs[g][there, at, :]
+                own_kept[g][free, at, :] = group_refs[g][here, at, :].astype(F32)
 
             strips(work)
-        own_copy(0).start()
+        own_copy(g, 0).start()
 
     def later(step, kept_ref, got_ref, sent_ref, q):
         for free in range(fsdp >> (step + 2)):
@@ -1114,21 +1120,24 @@
 
         strips(work)
 
-    def own_step(step):
-        own_copy(step).wait_recv()
+    def own_step(g, step):
+        own_copy(g, step).wait_recv()
         if step + 1 < levels:
-            later(step, own_kept, own_got[step], own_sent[step + 1], 0)
-            own_copy(step + 1).start()
+            later(step, own_kept[g], own_got[g][step], own_sent[g][step + 1], g)
+            own_copy(g, step + 1).start()
             return
 
         def place(at, value):
-            own_low[at, :] = value[:, : head + tail].astype(BF16)
-            beside[at, :] = value[:, head + tail :]
-
-        last(own_kept, own_got[step], 0, place)
-        for copy in far_copies:
-            copy.start()
-        own_start()
+            if g == 0:
+                beside[at, :] = value
+            else:
+                own_low[at, :] = value.astype(BF16)
+
+        last(own_kept[g], own_got[g][step], g, place)
+        if g == 1:
+            for copy in far_copies:
+                copy.start()
+            own_start()
 
     head = own_out.shape[2]
     tail = last_out.shape[2]
@@ -1237,7 +1246,8 @@
 
         gathers[b][0]()
 
-    own_begin()
+    own_begin(0)
+    own_begin(1)
     waiting = []
 
     def one_more():
@@ -1254,7 +1264,8 @@
     for b in range(batches - 1):
         batch(b)
     for step in range(levels):
-        own_step(step)
+        own_step(0, step)
+        own_step(1, step)
         one_more()
     waiting.extend(own_steps)
     batch(batches - 1)
@@ -1266,7 +1277,8 @@
     far_copies[2].wait()
     own_end()
     for step in range(levels):
-        own_copy(step).wait_send()
+        own_copy(0, step).wait_send()
+        own_copy(1, step).wait_send()
     for b in range(batches):
         gathers[b][2]()
         for chip in range(chips):
@@ -1278,37 +1290,37 @@
                         z_copy(side, z_last(side, chip) - 1, b).wait_send()
 
 
-def sum_grads(ctx, fsdp, pieces, own, head, tail):
+def sum_grads(ctx, fsdp, pieces, out, own, head):
     levels, chips = bits_of(fsdp), ctx // 2
     rows, units = pieces[0].shape
-    rest = own.shape[-1] - head - tail
-    whole = units + rest // 2
+    beside, own_width = out.shape[-1], own.shape[-1]
+    whole = units + beside // 2
     batches = max(n for n in range(1, 3) if whole % n == 0 and 2 * whole // n % (chips * 128) == 0)
     width = whole // batches
     chunk = 2 * width // chips
-    own_width = own.shape[-1]
     vmem = pl.BlockSpec(memory_space=pltpu.VMEM)
     dma = pltpu.SemaphoreType.DMA
     steps = [fsdp >> (i + 1) for i in range(levels)]
     result = jax.ShapeDtypeStruct((2, rows, whole), BF16)
     mine, other, own_all, last = pl.pallas_call(
         functools.partial(sum_kernel, ctx, fsdp, batches),
-        in_specs=[vmem] * 3,
+        in_specs=[vmem] * 4,
         out_specs=[vmem] * 4,
         out_shape=[
             result,
             result,
             jax.ShapeDtypeStruct((ctx, rows, head), BF16),
-            jax.ShapeDtypeStruct((2, rows, tail), BF16),
+            jax.ShapeDtypeStruct((2, rows, own_width - head), BF16),
         ],
         scratch_shapes=[
+            pltpu.VMEM((fsdp // 2, rows, beside), F32),
             pltpu.VMEM((fsdp // 2, rows, own_width), F32),
-            pltpu.VMEM((rows, head + tail), BF16),
-            pltpu.VMEM((rows, rest), F32),
+            pltpu.VMEM((rows, own_width), BF16),
+            pltpu.VMEM((rows, beside), F32),
         ]
-        + [pltpu.VMEM((n, rows, own_width), BF16) for n in steps * 2]
+        + [pltpu.VMEM((n, rows, size), BF16) for size in (beside, own_width) * 2 for n in steps]
         + [pltpu.VMEM((2, batches, chips - 1, rows, chunk), BF16)] * 2
-        + [dma((levels,))] * 2
+        + [dma((2, levels))] * 2
         + [dma((2, batches, chips - 1))] * 4
         + [dma((2, batches, chips))] * 2
         + [dma((2, chips - 1))] * 2
@@ -1319,7 +1331,7 @@
             collective_id=1, has_side_effects=True, vmem_limit_bytes=60 * 2**20
         ),
         cost_estimate=pl.CostEstimate(flops=1000, bytes_accessed=1000, transcendentals=0),
-    )(*pieces, own)
+    )(*pieces, out, own)
 
     return mine, other, own_all, last
 
@@ -1573,8 +1585,7 @@
         [
             jnp.pad(part, ((0, 0), (0, -part.shape[1] % 128)))
             for part in (own_sum[:, : regular * feat], own_sum[:, regular * feat :])
-        ]
-        + [out_total[0], out_total[1]],
+        ],
         axis=1,
     )
     head_columns = regular * feat + -regular * feat % 128
@@ -1583,9 +1594,9 @@
         ctx,
         fsdp,
         [up_part, down_part],
+        jnp.concatenate([out_total[0], out_total[1]], axis=1).reshape(*blocks, -1),
         own_sum.reshape(*blocks, own_sum.shape[1]),
         head_columns,
-        feat + -feat % 128,
     )
     first_rows, other_rows = to_rows(first_heads), to_rows(other_heads, sum_mine)
     last_rows = last_to_rows(last_heads, sum_mine)

time: 577 us -> 569 us (0.986)
  Pallas kernels: 395 us -> 386 us
    pallas_call x1, Pallas kernels: 121 us -> 112 us  [sum_grads(): pl.pallas_call(functools.partial(sum_kernel, ctx, fsdp, batches), in_spec...]
  transfers between devices with their start and end apart: 20 -> 20, of which waited for: 8 -> 8; matrix products, arithmetic and copies ran while one was open for 10% -> 10% of each run, Pallas kernels for 48% -> 47%
where the time goes in v2:
time: 569 us; the launch traced here: 559 us
  Pallas kernels  386 us (68%)
  other arithmetic  38.1 us (7%)
  starting transfers between devices  33.2 us (6%)
  local copies, waits for them, and re-layouts  24.7 us (4%)
  matrix products  21.2 us (4%)
  waiting for transfers between devices  20.6 us (4%)
  blocking collectives  20.2 us (4%)
  between operations  15.1 us (3%)
    pallas_call x1, Pallas kernels, sum_grads(): pl.pallas_call(functools.partial(sum_kernel, ctx, fsdp, batches), in_spec...  112 us
    pallas_call x1, Pallas kernels, gather_first(): pl.pallas_call(functools.partial(gather_kernel, ctx, fsdp, regular), in_s...  96.2 us
    pallas_call x2, Pallas kernels, mlp(): pl.pallas_call(functools.partial(mlp_kernel, units), grid=(pl.cdiv(units,...  50.6 us
    pallas_call x3, Pallas kernels, attend_back(): pl.pallas_call(functools.partial(attend_back_kernel, block), grid_spec=pl...  46.4 us
    pallas_call x1, Pallas kernels, update(): pl.pallas_call(functools.partial(update_kernel, units, regular), grid=(ro...  36.4 us
    pallas_call x3, Pallas kernels, attend(): pl.pallas_call(functools.partial(attend_kernel, block), grid_spec=pltpu.P...  31.7 us
    all_to_all x1, blocking collectives, body(): first_pairs = lax.all_to_all(first_send, 'ctx', 0, 0)  20.2 us
    all_to_all x4, starting transfers between devices, to_rows(): got = lax.all_to_all(array, 'ctx', 0, 0)  17.8 us
  transfers between devices with their start and end apart: 20, of which 8 were waited for; matrix products, arithmetic and copies ran while one was open for 10% of the time, Pallas kernels for 47%

profile of v2, /device:TPU:0, one launch (start us, length us, event | category | flops | bytes accessed | tf_op | source)
XLA Modules:
  0.0 559.3 jit_solution(15510119558643227812)
XLA Ops:
  8.1 2.8 fusion.19
  11.6 96.2 %shard_map.203 = (bf16[2,8,1088,256]{3,2,1,0:T(8,128)(2,1)}, bf16[2,576,2048]{2,1,0:T(8,128)(2,1)}, bf16[4,272,4352]{2,1,0:T(8,128)(2,1)}, bf16[4,272,2176]{2,1,...) custom-call(bf16[2,1088,256]{2,1,0:T(8,128)(2,1)} %bitcast.156, f32[272,8704]{1,0:T(8,128)} %refs_0_.1, ...), custom_call_target="tpu_custom_call" | custom-call | flops 1000 | bytes 1000 | tf_op jit(solution)/shard_map/pallas_call | solution.py:835
  109.1 12.5 %shard_map.204 = (f32[2,64,2048]{2,1,0:T(8,128)S(1)}, bf16[8,2,64,256]{3,2,1,0:T(8,128)(2,1)}, f32[2,1,2048]{2,1,0:T(1,128)S(1)}) custom-call(s32[2]{0:T(128)S(1)} %reshape.211.lens_ref, bf16[2,3,3,64,2048]{4,3,2,1,0:T(8,128)(2,1)} %bitcast.143, bf16[2,3,3,64,2048]{4,3,2,1,0:T(8,128)(2,1)} %bitcast.144, bf16[2,3,3,64,2048]{4,3,2,1,0:T(8,128)(2,1)} %bitcast.145), custom_call_target="tpu_custom_call" | custom-call | flops 1000 | bytes 1000 | tf_op jit(solution)/shard_map/pallas_call | solution.py:114
  122.6 4.8 all-to-all-start
  128.0 12.1 %shard_map.205 = (f32[2,64,2048]{2,1,0:T(8,128)S(1)}, bf16[8,2,64,256]{3,2,1,0:T(8,128)(2,1)}, f32[2,1,2048]{2,1,0:T(1,128)S(1)}) custom-call(s32[2]{0:T(128)S(1)} %reshape.214.lens_ref, bf16[2,3,3,64,2048]{4,3,2,1,0:T(8,128)(2,1)} %bitcast.146, bf16[2,3,3,64,2048]{4,3,2,1,0:T(8,128)(2,1)} %bitcast.147, bf16[2,3,3,64,2048]{4,3,2,1,0:T(8,128)(2,1)} %bitcast.148), custom_call_target="tpu_custom_call" | custom-call | flops 1000 | bytes 1000 | tf_op jit(solution)/shard_map/pallas_call | solution.py:114
  140.2 2.6 all-to-all-done
  142.7 4.1 all-to-all-start.1
  146.9 1.5 slice_select_fusion.q_ref.k_ref.v_ref
  148.4 7.1 %shard_map.206 = (f32[1,64,2048]{2,1,0:T(8,128)S(1)}, bf16[8,1,64,256]{3,2,1,0:T(8,128)(2,1)S(1)}, f32[1,1,2048]{2,1,0:T(1,128)S(1)}) custom-call(s32[1]{0:T(128)} %get-tuple-element.64.lens_ref, bf16[1,3,1,64,2048]{4,3,2,1,0:T(8,128)(2,1)S(1)} %slice_select_fusion.q_ref.k_ref.v_ref, bf16[1,3,1,64,2048]{4,3,2,1,0:T(8,128)(2,1)S(1)} %slice_select_fusion.q_ref.k_ref.v_ref, ...), custom_call_target="tpu_custom_call" | custom-call | flops 1000 | bytes 1000 | tf_op jit(solution)/shard_map/pallas_call | solution.py:114
  155.6 6.7 %all-to-all-done.1 = bf16[8,2,64,256]{3,2,1,0:T(8,128)(2,1)} async-done(((bf16[8,2,64,256]{3,2,1,0:T(8,128)(2,1)}), bf16[8,2,64,256]{3,2,1,0:T(8,128)(2,1)}, u32[]{:S(2)}, u32[]{:S(2)}) %all-to-all-start.1) | async-done | bytes 524320 | tf_op jit(solution)/shard_map/all_to_all | solution.py:1483
  162.2 1.9 copy.66
  164.1 1.4 all-gather.2.cloned.1.call-done.down_ref
  166.9 2.5 convert_reduce_fusion.2
  170.6 2.4 collective-permute-start
  173.1 2.7 collective-permute-done
  177.7 4.9 fusion.42
  182.9 1.4 add_convert_fusion.3.a_ref
  184.4 25.2 %shard_map.208 = (f32[2,1088,256]{2,1,0:T(8,128)}, f32[2,1088,256]{2,1,0:T(8,128)}, bf16[1088,2176]{1,0:T(8,128)(2,1)}, bf16[1088,2176]{1,0:T(8,128)(2,1)}, f32[1,2176]{1,0:T(1,128)}) custom-call(bf16[2,1088,256]{2,1,0:T(8,128)(2,1)} %add_convert_fusion.3.a_ref, bf16[2,1088,256]{2,1,0:T(8,128)(2,1)} %get-tuple-element.123.g_ref, ...), custom_call_target="tpu_custom_call" | custom-call | flops 1000 | bytes 1000 | tf_op jit(solution)/shard_map/pallas_call | solution.py:369
  209.6 25.4 %shard_map.207 = (f32[2,1088,256]{2,1,0:T(8,128)}, f32[2,1088,256]{2,1,0:T(8,128)}, bf16[1088,2176]{1,0:T(8,128)(2,1)}, bf16[1088,2176]{1,0:T(8,128)(2,1)}, f32[1,2176]{1,0:T(1,128)}) custom-call(bf16[2,1088,256]{2,1,0:T(8,128)(2,1)} %add_convert_fusion.3.a_ref, bf16[2,1088,256]{2,1,0:T(8,128)(2,1)} %get-tuple-element.123.g_ref, ...), custom_call_target="tpu_custom_call" | custom-call | flops 1000 | bytes 1000 | tf_op jit(solution)/shard_map/pallas_call | solution.py:369
  235.0 5.7 %add_convert_fusion.1 = bf16[1088,2176]{1,0:T(8,128)(2,1)} fusion(bf16[1088,2176]{1,0:T(8,128)(2,1)S(1)} %collective-permute-done.2, bf16[1088,2176]{1,0:T(8,128)(2,1)} %get-tuple-element.78), kind=kLoop, calls=%fused_computation.1 | loop fusion | flops 9469952 | bytes 14204928 | tf_op jit(solution)/shard_map/convert_element_type | solution.py:902
  241.3 4.9 multiply_reduce_fusion
  247.5 4.1 convolution_convert_fusion
  251.8 20.2 %all_to_all.30.grad_ref = bf16[8,2,64,256]{3,2,1,0:T(8,128)(2,1)S(1)} all-to-all(bf16[8,2,64,256]{3,2,1,0:T(8,128)(2,1)S(1)} %bitcast.179), channel_id=1, replica_groups=mesh['ctx'=8,'fsdp'=4] {'ctx'}, dimensions={0} | all-to-all | bytes 1048576 | tf_op jit(solution)/shard_map/all_to_all | solution.py:1547
  272.0 3.5 add_convert_fusion
  277.4 4.4 all-to-all-start.4
  281.8 1.3 copy-done.1
  283.1 18.6 %shard_map.209 = bf16[8,2,192,256]{3,2,1,0:T(8,128)(2,1)} custom-call(s32[2]{0:T(128)S(1)} %reshape.211.lens_ref, bf16[2,3,3,64,2048]{4,3,2,1,0:T(8,128)(2,1)} %bitcast.150, bf16[2,3,3,64,2048]{4,3,2,1,0:T(8,128)(2,1)} %bitcast.151, bf16[2,3,3,64,2048]{4,3,2,1,0:T(8,128)(2,1)} %bitcast.152, f32[2,64,2048]{2,1,0:T(8,128)S(1)} %copy-done.1, ...), custom_call_target="tpu_custom_call" | custom-call | flops 1000 | bytes 1000 | tf_op jit(solution)/shard_map/pallas_call | solution.py:220
  302.8 4.3 all-to-all-start.3
  307.1 3.2 bitcast_convert_fusion
  310.3 2.1 constant_dynamic-slice_fusion.4
  314.9 9.2 %shard_map.210 = bf16[8,1,192,256]{3,2,1,0:T(8,128)(2,1)S(1)} custom-call(s32[1]{0:T(128)} %get-tuple-element.64.lens_ref, bf16[1,3,1,64,2048]{4,3,2,1,0:T(8,128)(2,1)S(1)} %slice_select_fusion.q_ref.k_ref.v_ref, bf16[1,3,1,64,2048]{4,3,2,1,0:T(8,128)(2,1)S(1)} %slice_select_fusion.q_ref.k_ref.v_ref, ...), custom_call_target="tpu_custom_call" | custom-call | flops 1000 | bytes 1000 | tf_op jit(solution)/shard_map/pallas_call | solution.py:220
  325.3 18.6 %shard_map.211 = bf16[8,2,192,256]{3,2,1,0:T(8,128)(2,1)} custom-call(s32[2]{0:T(128)S(1)} %reshape.214.lens_ref, bf16[2,3,3,64,2048]{4,3,2,1,0:T(8,128)(2,1)} %bitcast.153, bf16[2,3,3,64,2048]{4,3,2,1,0:T(8,128)(2,1)} %bitcast.154, bf16[2,3,3,64,2048]{4,3,2,1,0:T(8,128)(2,1)} %bitcast.155, f32[2,64,2048]{2,1,0:T(8,128)S(1)} %get-tuple-element.63.o_ref, ...), custom_call_target="tpu_custom_call" | custom-call | flops 1000 | bytes 1000 | tf_op jit(solution)/shard_map/pallas_call | solution.py:220
  344.9 4.6 all-to-all-start.5
  350.0 1.9 fusion.1
  352.0 1.3 pad_maximum_fusion.2.refs_2_
  353.3 2.9 collective-permute-start.3
  356.2 1.5 copy.75
  357.8 13.0 %shard_map.212 = f32[1088,576]{1,0:T(8,128)} custom-call(s32[1]{0:T(128)} %bitcast.48.late_ref, bf16[2,8,1088,256]{3,2,1,0:T(8,128)(2,1)} %get-tuple-element.90.first_ref.second_ref, bf16[2,8,1088,256]{3,2,1,0:T(8,128)(2,1)} %get-tuple-element.90.first_ref.second_ref, bf16[8,384,256]{2,1,0:T(8,128)(2,1)} %bitcast.49.first_grad_ref, ...), custom_call_target="tpu_custom_call" | custom-call | flops 1000 | bytes 1000 | tf_op jit(solution)/shard_map/pallas_call | solution.py:283
  370.8 1.9 convert_element_type.123
  372.9 1.2 fusion.18
  374.1 112.0 %shard_map.213 = (bf16[2,272,2560]{2,1,0:T(8,128)(2,1)}, bf16[2,272,2560]{2,1,0:T(8,128)(2,1)}, bf16[8,272,384]{2,1,0:T(8,128)(2,1)}, bf16[2,272,256]{2,1,0:T(8,128)(2,1)}) custom-call(bf16[272,2176]{1,0:T(8,128)(2,1)} %reduce-scatter.7.cloned.1.call-done.refs_0_, bf16[272,2176]{1,0:T(8,128)(2,1)} %reduce-scatter.9.cloned.1.call-done.refs_1_, ...), custom_call_target="tpu_custom_call" | custom-call | flops 1000 | bytes 1000 | tf_op jit(solution)/shard_map/pallas_call | solution.py:1305
  486.4 2.1 copy.79
  490.7 9.0 %fusion.14 = (f32[1088]{0:T(1024)S(1)}, f32[2,256]{1,0:T(2,128)}, f32[2,256]{1,0:T(2,128)}, f32[2,256,1088]{1,2,0:T(8,128)S(1)}) fusion(f32[2,256]{1,0:T(2,128)S(1)} %add_rsqrt_fusion, f32[2,256]{1,0:T(2,128)S(1)} %copy-done.29, bf16[256,2,1088]{0,2,1:T(8,128)(2,1)S(1)} %copy-done.11, f32[1088]{0:T(1024)S(1)} %get-tuple-element.114, ...), kind=kOutput, calls=%fused_computation.31 | convolution fusion | flops 3648157696 | bytes 13943296 | tf_op jit(solution)/shard_map/de,set->sdt/dot_general | solution.py:1609
  500.5 1.6 collective-permute-start.6
  504.1 36.4 %shard_map.214 = (f32[272,8704]{1,0:T(8,128)}, f32[272,8704]{1,0:T(8,128)}, f32[272,8704]{1,0:T(8,128)}, f32[272,4352]{1,0:T(8,128)}, f32[272,4352]{1,0:T(8,128)}, /*index=5*/f32[272,4352]{1,0:T(8,128)}) custom-call(f32[272,8704]{1,0:T(8,128)} %refs_0_.1, bf16[272,8704]{1,0:T(8,128)(2,1)} %refs_1_.1, f32[272,8704]{1,0:T(8,128)} %refs_2_.1, ...), custom_call_target="tpu_custom_call" | custom-call | flops 1000 | bytes 1000 | tf_op jit(solution)/shard_map/pallas_call | solution.py:1425
  540.6 1.2 collective-permute-done.9
  541.8 3.8 collective-permute-done.10
  546.7 4.9 fusion.21
  (186 shorter events, 26.9 us)
Async XLA Ops:
  7.2 158.4 %all-gather.2.cloned.1.call-start = ((), (), s32[]{:S(2)}) async-start(), calls=%async_computation.8 | async-start | bytes 5918720 | tf_op jit(solution)/shard_map/all_gather | solution.py:1474
  11.6 96.2 %copy-start.35 = (s32[2]{0:T(128)S(1)}, s32[2]{0:T(128)}, u32[]{:S(2)}) copy-start(s32[2]{0:T(128)} %param.14) | copy-start | bytes 28
  122.6 20.1 %all-to-all-start = ((bf16[8,2,64,256]{3,2,1,0:T(8,128)(2,1)}), bf16[8,2,64,256]{3,2,1,0:T(8,128)(2,1)S(1)}, u32[]{:S(2)}, u32[]{:S(2)}) async-start(bf16[8,2,64,256]{3,2,1,0:T(8,128)(2,1)} %get-tuple-element.60), calls=%async_computation | async-start | bytes 1048576 | tf_op jit(solution)/shard_map/all_to_all | solution.py:1483
  142.7 19.5 %all-to-all-start.1 = ((bf16[8,2,64,256]{3,2,1,0:T(8,128)(2,1)}), bf16[8,2,64,256]{3,2,1,0:T(8,128)(2,1)}, u32[]{:S(2)}, u32[]{:S(2)}) async-start(bf16[8,2,64,256]{3,2,1,0:T(8,128)(2,1)} %get-tuple-element.66), calls=%async_computation.1 | async-start | bytes 1048576 | tf_op jit(solution)/shard_map/all_to_all | solution.py:1483
  146.9 178.4 %reduce-scatter.7.cloned.1.call-start = ((), (), s32[]{:S(2)}) async-start(), calls=%async_computation.9 | async-start | bytes 5918720
  165.5 18.8 %collective-permute-start.1 = (bf16[1088,2176]{1,0:T(8,128)(2,1)}, bf16[1088,2176]{1,0:T(8,128)(2,1)}, u32[]{:S(2)}, u32[]{:S(2)}) collective-permute-start(bf16[1088,2176]{1,0:T(8,128)(2,1)} %all-gather.2.cloned.1.call-done.down_ref), channel_id=1, source_target_pairs={{0,4},{4,0},{8,12},{12,8},{16,20},{20,16},{24,28},{28,24},{1,5},{5... | collective-permute-start | bytes 14204936 | tf_op jit(solution)/shard_map/ppermute | solution.py:1340
  170.6 5.1 collective-permute-start
  173.0 4.6 copy-start.9
  177.7 5.0 copy-start.19
  177.7 5.0 copy-start.20
  209.6 25.4 %collective-permute-start.2 = (bf16[1088,2176]{1,0:T(8,128)(2,1)}, bf16[1088,2176]{1,0:T(8,128)(2,1)S(1)}, u32[]{:S(2)}, u32[]{:S(2)}) collective-permute-start(bf16[1088,2176]{1,0:T(8,128)(2,1)} %get-tuple-element.79), channel_id=1, source_target_pairs={{0,4},{4,0},{8,12},{12,8},{16,20},{20,16},{24,28},{28,24},{1,5},{5... | collective-permute-start | bytes 14204936 | tf_op jit(solution)/shard_map/ppermute | solution.py:1340
  240.7 133.4 %reduce-scatter.9.cloned.1.call-start = ((), (), s32[]{:S(2)}) async-start(), calls=%async_computation.10 | async-start | bytes 5918720
  240.7 31.2 %collective-permute-start.4 = (bf16[1088,2176]{1,0:T(8,128)(2,1)}, bf16[1088,2176]{1,0:T(8,128)(2,1)S(1)}, u32[]{:S(2)}, u32[]{:S(2)}) collective-permute-start(bf16[1088,2176]{1,0:T(8,128)(2,1)} %get-tuple-element.88), channel_id=1, source_target_pairs={{0,4},{4,0},{8,12},{12,8},{16,20},{20,16},{24,28},{28,24},{1,5},{5... | collective-permute-start | bytes 14204936 | tf_op jit(solution)/shard_map/ppermute | solution.py:1340
  241.3 4.9 copy-start.3
  241.3 4.9 copy-start.5
  247.5 24.5 %slice-start = ((s8[4734976]{0:T(1024)(128)(4,1)}), s8[4194304]{0:T(1024)(128)(4,1)S(1)}, s32[]{:S(2)}) async-start(s8[4734976]{0:T(1024)(128)(4,1)} %bitcast.169), calls=%async_computation.11 | async-start | bytes 8388608
  247.5 24.5 %slice-start.1 = ((s8[4734976]{0:T(1024)(128)(4,1)}), s8[540672]{0:T(1024)(128)(4,1)S(1)}, s32[]{:S(2)}) async-start(s8[4734976]{0:T(1024)(128)(4,1)} %bitcast.169), calls=%async_computation.12 | async-start | bytes 1081344
  251.6 20.3 %copy-start.18 = (bf16[2,256,1088]{1,2,0:T(8,128)(2,1)}, bf16[2,256,1088]{1,2,0:T(8,128)(2,1)S(1)}, u32[]{:S(2)}) copy-start(bf16[2,256,1088]{1,2,0:T(8,128)(2,1)S(1)} %convolution_convert_fusion) | copy-start | bytes 3342340
  277.4 25.4 %all-to-all-start.4 = ((bf16[8,3,64,256]{3,2,1,0:T(8,128)(2,1)}), bf16[8,3,64,256]{3,2,1,0:T(8,128)(2,1)}, u32[]{:S(2)}, u32[]{:S(2)}) async-start(bf16[8,3,64,256]{3,2,1,0:T(8,128)(2,1)} %pad_maximum_fusion.4), calls=%async_computation.4 | async-start | bytes 1572864 | tf_op jit(solution)/shard_map/all_to_all | solution.py:1549
  301.7 5.4 copy-start.17
  302.8 42.2 %all-to-all-start.3 = ((bf16[8,2,192,256]{3,2,1,0:T(8,128)(2,1)}), bf16[8,2,192,256]{3,2,1,0:T(8,128)(2,1)}, u32[]{:S(2)}, u32[]{:S(2)}) async-start(bf16[8,2,192,256]{3,2,1,0:T(8,128)(2,1)} %shard_map.209), calls=%async_computation.3 | async-start | bytes 3145728 | tf_op jit(solution)/shard_map/all_to_all | solution.py:1483
  312.4 37.6 %collective-permute-start.5 = (bf16[2,1088,384]{2,1,0:T(8,128)(2,1)}, bf16[2,1088,384]{2,1,0:T(8,128)(2,1)}, u32[]{:S(2)}, u32[]{:S(2)}) collective-permute-start(bf16[2,1088,384]{2,1,0:T(8,128)(2,1)} %bitcast.45), channel_id=1, source_target_pairs={{0,4},{4,0},{8,12},{12,8},{16,20},{20,16},{24,28},{28,24},{1,5},{5... | collective-permute-start | bytes 5013512 | tf_op jit(solution)/shard_map/ppermute | solution.py:1340
  313.6 10.5 %copy-start.28 = (f32[2,256]{1,0:T(2,128)}, f32[2,256]{1,0:T(2,128)S(1)}, u32[]{:S(2)}) copy-start(f32[2,256]{1,0:T(2,128)S(1)} %broadcast_multiply_fusion.2) | copy-start | bytes 6148
  314.0 176.1 %copy-start.33 = (f32[2,256]{1,0:T(2,128)}, f32[2,256]{1,0:T(2,128)S(1)}, u32[]{:S(2)}) copy-start(f32[2,256]{1,0:T(2,128)S(1)} %add_rsqrt_fusion) | copy-start | bytes 6148
  343.8 5.7 %copy-start.31 = (f32[1,2176]{1,0:T(1,128)S(1)}, f32[1,2176]{1,0:T(1,128)}, u32[]{:S(2)}) copy-start(f32[1,2176]{1,0:T(1,128)} %get-tuple-element.106) | copy-start | bytes 26116
  343.8 5.7 %copy-start.32 = (f32[1,2176]{1,0:T(1,128)S(1)}, f32[1,2176]{1,0:T(1,128)}, u32[]{:S(2)}) copy-start(f32[1,2176]{1,0:T(1,128)} %get-tuple-element.105) | copy-start | bytes 26116
  343.8 5.9 %copy-start.23 = (f32[1088]{0:T(1024)S(1)}, f32[1088]{0:T(1024)}, u32[]{:S(2)}) copy-start(f32[1088]{0:T(1024)} %get-tuple-element.107) | copy-start | bytes 13060
  343.8 6.0 %copy-start.22 = (f32[1088]{0:T(1024)S(1)}, f32[1088]{0:T(1024)}, u32[]{:S(2)}) copy-start(f32[1088]{0:T(1024)} %get-tuple-element.113) | copy-start | bytes 13060
  343.9 6.1 %copy-start.13 = (bf16[1,2,4,272,384]{4,3,2,1,0:T(8,128)(2,1)S(1)}, bf16[1,2,4,272,384]{4,3,2,1,0:T(8,128)(2,1)}, u32[]{:S(2)}) copy-start(bf16[1,2,4,272,384]{4,3,2,1,0:T(8,128)(2,1)} %get-tuple-element.128) | copy-start | bytes 5013508
  344.9 141.5 %all-to-all-start.5 = ((bf16[8,2,192,256]{3,2,1,0:T(8,128)(2,1)}), bf16[8,2,192,256]{3,2,1,0:T(8,128)(2,1)}, u32[]{:S(2)}, u32[]{:S(2)}) async-start(bf16[8,2,192,256]{3,2,1,0:T(8,128)(2,1)} %shard_map.211), calls=%async_computation.5 | async-start | bytes 3145728 | tf_op jit(solution)/shard_map/all_to_all | solution.py:1483
  353.3 132.8 %collective-permute-start.3 = (bf16[1,192,256]{2,1,0:T(8,128)(2,1)S(1)}, bf16[1,192,256]{2,1,0:T(8,128)(2,1)S(1)}, u32[]{:S(2)}, u32[]{:S(2)}) collective-permute-start(bf16[1,192,256]{2,1,0:T(8,128)(2,1)S(1)} %dynamic-slice_bitcast_fusion), channel_id=1, source_target_pairs={{0,16},{4,20},{8,24},{12,28},{16,0},{20,4},{24,8},{28,12},{1,17},{... | collective-permute-start | bytes 294920 | tf_op jit(solution)/shard_map/ppermute | solution.py:1489
  499.7 4.4 copy-start.12
  500.5 40.0 %collective-permute-start.6 = (f32[12,272]{1,0:T(8,128)S(1)}, f32[12,272]{1,0:T(8,128)S(1)}, u32[]{:S(2)}, u32[]{:S(2)}) collective-permute-start(f32[12,272]{1,0:T(8,128)S(1)} %bitcast.194), channel_id=1, source_target_pairs={{0,1},{1,0},{2,3},{3,2},{4,5},{5,4},{6,7},{7,6},{8,9},{9,8},{10,11... | collective-permute-start | bytes 39176 | tf_op jit(solution)/shard_map/ppermute | solution.py:1635
  502.1 38.4 %collective-permute-start.7 = (f32[12,272]{1,0:T(8,128)S(1)}, f32[12,272]{1,0:T(8,128)S(1)}, u32[]{:S(2)}, u32[]{:S(2)}) collective-permute-start(f32[12,272]{1,0:T(8,128)S(1)} %bitcast.195), channel_id=1, source_target_pairs={{0,2},{1,3},{2,0},{3,1},{4,6},{5,7},{6,4},{7,5},{8,10},{9,11},{10,... | collective-permute-start | bytes 39176 | tf_op jit(solution)/shard_map/ppermute | solution.py:1635
  503.1 37.4 %collective-permute-start.8 = (f32[12,272]{1,0:T(8,128)S(1)}, f32[12,272]{1,0:T(8,128)S(1)}, u32[]{:S(2)}, u32[]{:S(2)}) collective-permute-start(f32[12,272]{1,0:T(8,128)S(1)} %bitcast.196), channel_id=1, source_target_pairs={{0,3},{1,2},{2,1},{3,0},{4,7},{5,6},{6,5},{7,4},{8,11},{9,10},{10,... | collective-permute-start | bytes 39176 | tf_op jit(solution)/shard_map/ppermute | solution.py:1635
  504.1 36.5 %copy-start.37 = (f32[2,256]{1,0:T(2,128)S(1)}, f32[2,256]{1,0:T(2,128)}, u32[]{:S(2)}) copy-start(f32[2,256]{1,0:T(2,128)} %get-tuple-element.110) | copy-start | bytes 6148
  504.1 37.7 %copy-start.36 = (f32[2,256]{1,0:T(2,128)S(1)}, f32[2,256]{1,0:T(2,128)}, u32[]{:S(2)}) copy-start(f32[2,256]{1,0:T(2,128)} %get-tuple-element.111) | copy-start | bytes 6148
  504.1 42.6 %copy-start.4 = (f32[2,1088,256]{2,1,0:T(8,128)S(1)}, f32[2,1088,256]{2,1,0:T(8,128)}, u32[]{:S(2)}) copy-start(f32[2,1088,256]{2,1,0:T(8,128)} %copy-done.2) | copy-start | bytes 6684676
  504.1 42.6 %copy-start.6 = (bf16[2,1088,256]{2,1,0:T(8,128)(2,1)S(1)}, bf16[2,1088,256]{2,1,0:T(8,128)(2,1)}, u32[]{:S(2)}) copy-start(bf16[2,1088,256]{2,1,0:T(8,128)(2,1)} %get-tuple-element.123.g_ref) | copy-start | bytes 3342340
  504.1 42.6 %copy-start.8 = (f32[2,1088,256]{2,1,0:T(8,128)S(1)}, f32[2,1088,256]{2,1,0:T(8,128)}, u32[]{:S(2)}) copy-start(f32[2,1088,256]{2,1,0:T(8,128)} %copy-done.7) | copy-start | bytes 6684676
  504.1 42.6 %copy-start.27 = (f32[2,256]{1,0:T(2,128)S(1)}, f32[2,256]{1,0:T(2,128)}, u32[]{:S(2)}) copy-start(f32[2,256]{1,0:T(2,128)} %copy-done.26) | copy-start | bytes 6148
  504.1 42.6 %copy-start.34 = (f32[2,256]{1,0:T(2,128)S(1)}, f32[2,256]{1,0:T(2,128)}, u32[]{:S(2)}) copy-start(f32[2,256]{1,0:T(2,128)} %copy-done.33) | copy-start | bytes 6148
  540.5 1.3 collective-permute-start.9
  541.8 3.8 collective-permute-start.10
  545.6 6.0 %collective-permute-start.11 = (f32[12,272]{1,0:T(8,128)S(1)}, f32[12,272]{1,0:T(8,128)S(1)}, u32[]{:S(2)}, u32[]{:S(2)}) collective-permute-start(f32[12,272]{1,0:T(8,128)S(1)} %add.229), channel_id=1, source_target_pairs={{0,16},{4,20},{8,24},{12,28},{16,0},{20,4},{24,8},{28,12},{1,17},{... | collective-permute-start | bytes 39176 | tf_op jit(solution)/shard_map/ppermute | solution.py:1637
  546.7 4.9 copy-start.21
  546.7 4.9 copy-start.25
  546.7 4.9 copy-start.30
  (12 other events, 22.0 us)
Sparse Core Ops, SparseCore 0:
  107.9 57.5 all-gather.1
  240.8 59.3 reduce-scatter.6
  304.1 58.6 reduce-scatter.8

commit v3 on v2

--- a/solution.py
+++ b/solution.py
@@ -357,7 +357,7 @@
 def mlp(act, grad, up, down, bias):
     slots, width, tok = act.shape
     units = up.shape[1]
-    block = 256
+    block = 512
 
     def fixed(shape):
         return pl.BlockSpec(shape, lambda i: (0,) * len(shape))

time: 569 us -> 566 us (level)
  no operation moved by 1% of the time
where the time goes in v3:
time: 566 us; the launch traced here: 556 us
  Pallas kernels  383 us (68%)
  other arithmetic  38.1 us (7%)
  starting transfers between devices  33.9 us (6%)
  local copies, waits for them, and re-layouts  24.7 us (4%)
  matrix products  21.3 us (4%)
  blocking collectives  20.3 us (4%)
  waiting for transfers between devices  20.1 us (4%)
  between operations  14.8 us (3%)
    pallas_call x1, Pallas kernels, sum_grads(): pl.pallas_call(functools.partial(sum_kernel, ctx, fsdp, batches), in_spec...  112 us
    pallas_call x1, Pallas kernels, gather_first(): pl.pallas_call(functools.partial(gather_kernel, ctx, fsdp, regular), in_s...  96.2 us
    pallas_call x2, Pallas kernels, mlp(): pl.pallas_call(functools.partial(mlp_kernel, units), grid=(pl.cdiv(units,...  47.2 us
    pallas_call x3, Pallas kernels, attend_back(): pl.pallas_call(functools.partial(attend_back_kernel, block), grid_spec=pl...  46.4 us
    pallas_call x1, Pallas kernels, update(): pl.pallas_call(functools.partial(update_kernel, units, regular), grid=(ro...  36.4 us
    pallas_call x3, Pallas kernels, attend(): pl.pallas_call(functools.partial(attend_kernel, block), grid_spec=pltpu.P...  31.8 us
    all_to_all x1, blocking collectives, body(): first_pairs = lax.all_to_all(first_send, 'ctx', 0, 0)  20.3 us
    all_to_all x4, starting transfers between devices, to_rows(): got = lax.all_to_all(array, 'ctx', 0, 0)  18 us
  transfers between devices with their start and end apart: 20, of which 8 were waited for; matrix products, arithmetic and copies ran while one was open for 10% of the time, Pallas kernels for 47%

profile of v3, /device:TPU:0, one launch (start us, length us, event | category | flops | bytes accessed | tf_op | source)
XLA Modules:
  0.0 556.2 jit_solution(13539272978993186121)
XLA Ops:
  8.1 2.8 fusion.19
  11.6 96.2 %shard_map.203 = (bf16[2,8,1088,256]{3,2,1,0:T(8,128)(2,1)}, bf16[2,576,2048]{2,1,0:T(8,128)(2,1)}, bf16[4,272,4352]{2,1,0:T(8,128)(2,1)}, bf16[4,272,2176]{2,1,...) custom-call(bf16[2,1088,256]{2,1,0:T(8,128)(2,1)} %bitcast.156, f32[272,8704]{1,0:T(8,128)} %refs_0_.1, ...), custom_call_target="tpu_custom_call" | custom-call | flops 1000 | bytes 1000 | tf_op jit(solution)/shard_map/pallas_call | solution.py:835
  109.1 12.6 %shard_map.204 = (f32[2,64,2048]{2,1,0:T(8,128)S(1)}, bf16[8,2,64,256]{3,2,1,0:T(8,128)(2,1)}, f32[2,1,2048]{2,1,0:T(1,128)S(1)}) custom-call(s32[2]{0:T(128)S(1)} %reshape.211.lens_ref, bf16[2,3,3,64,2048]{4,3,2,1,0:T(8,128)(2,1)} %bitcast.143, bf16[2,3,3,64,2048]{4,3,2,1,0:T(8,128)(2,1)} %bitcast.144, bf16[2,3,3,64,2048]{4,3,2,1,0:T(8,128)(2,1)} %bitcast.145), custom_call_target="tpu_custom_call" | custom-call | flops 1000 | bytes 1000 | tf_op jit(solution)/shard_map/pallas_call | solution.py:114
  122.7 4.8 all-to-all-start
  128.1 12.1 %shard_map.205 = (f32[2,64,2048]{2,1,0:T(8,128)S(1)}, bf16[8,2,64,256]{3,2,1,0:T(8,128)(2,1)}, f32[2,1,2048]{2,1,0:T(1,128)S(1)}) custom-call(s32[2]{0:T(128)S(1)} %reshape.214.lens_ref, bf16[2,3,3,64,2048]{4,3,2,1,0:T(8,128)(2,1)} %bitcast.146, bf16[2,3,3,64,2048]{4,3,2,1,0:T(8,128)(2,1)} %bitcast.147, bf16[2,3,3,64,2048]{4,3,2,1,0:T(8,128)(2,1)} %bitcast.148), custom_call_target="tpu_custom_call" | custom-call | flops 1000 | bytes 1000 | tf_op jit(solution)/shard_map/pallas_call | solution.py:114
  140.3 2.6 all-to-all-done
  142.9 4.1 all-to-all-start.1
  147.1 1.5 slice_select_fusion.q_ref.k_ref.v_ref
  148.6 7.1 %shard_map.206 = (f32[1,64,2048]{2,1,0:T(8,128)S(1)}, bf16[8,1,64,256]{3,2,1,0:T(8,128)(2,1)S(1)}, f32[1,1,2048]{2,1,0:T(1,128)S(1)}) custom-call(s32[1]{0:T(128)} %get-tuple-element.64.lens_ref, bf16[1,3,1,64,2048]{4,3,2,1,0:T(8,128)(2,1)S(1)} %slice_select_fusion.q_ref.k_ref.v_ref, bf16[1,3,1,64,2048]{4,3,2,1,0:T(8,128)(2,1)S(1)} %slice_select_fusion.q_ref.k_ref.v_ref, ...), custom_call_target="tpu_custom_call" | custom-call | flops 1000 | bytes 1000 | tf_op jit(solution)/shard_map/pallas_call | solution.py:114
  155.7 6.7 %all-to-all-done.1 = bf16[8,2,64,256]{3,2,1,0:T(8,128)(2,1)} async-done(((bf16[8,2,64,256]{3,2,1,0:T(8,128)(2,1)}), bf16[8,2,64,256]{3,2,1,0:T(8,128)(2,1)}, u32[]{:S(2)}, u32[]{:S(2)}) %all-to-all-start.1) | async-done | bytes 524320 | tf_op jit(solution)/shard_map/all_to_all | solution.py:1483
  162.4 1.9 copy.66
  166.7 2.5 convert_reduce_fusion.2
  170.4 2.4 collective-permute-start
  172.9 2.6 collective-permute-done
  177.5 4.9 fusion.42
  182.8 1.4 add_convert_fusion.3.a_ref
  184.2 23.5 %shard_map.208 = (f32[2,1088,256]{2,1,0:T(8,128)}, f32[2,1088,256]{2,1,0:T(8,128)}, bf16[1088,2176]{1,0:T(8,128)(2,1)}, bf16[1088,2176]{1,0:T(8,128)(2,1)}, f32[1,2176]{1,0:T(1,128)}) custom-call(bf16[2,1088,256]{2,1,0:T(8,128)(2,1)} %add_convert_fusion.3.a_ref, bf16[2,1088,256]{2,1,0:T(8,128)(2,1)} %get-tuple-element.123.g_ref, ...), custom_call_target="tpu_custom_call" | custom-call | flops 1000 | bytes 1000 | tf_op jit(solution)/shard_map/pallas_call | solution.py:369
  207.7 23.7 %shard_map.207 = (f32[2,1088,256]{2,1,0:T(8,128)}, f32[2,1088,256]{2,1,0:T(8,128)}, bf16[1088,2176]{1,0:T(8,128)(2,1)}, bf16[1088,2176]{1,0:T(8,128)(2,1)}, f32[1,2176]{1,0:T(1,128)}) custom-call(bf16[2,1088,256]{2,1,0:T(8,128)(2,1)} %add_convert_fusion.3.a_ref, bf16[2,1088,256]{2,1,0:T(8,128)(2,1)} %get-tuple-element.123.g_ref, ...), custom_call_target="tpu_custom_call" | custom-call | flops 1000 | bytes 1000 | tf_op jit(solution)/shard_map/pallas_call | solution.py:369
  231.5 5.7 %add_convert_fusion.1 = bf16[1088,2176]{1,0:T(8,128)(2,1)} fusion(bf16[1088,2176]{1,0:T(8,128)(2,1)S(1)} %collective-permute-done.2, bf16[1088,2176]{1,0:T(8,128)(2,1)} %get-tuple-element.78), kind=kLoop, calls=%fused_computation.1 | loop fusion | flops 9469952 | bytes 14204928 | tf_op jit(solution)/shard_map/convert_element_type | solution.py:902
  237.8 4.9 multiply_reduce_fusion
  244.0 4.1 convolution_convert_fusion
  248.3 20.3 %all_to_all.30.grad_ref = bf16[8,2,64,256]{3,2,1,0:T(8,128)(2,1)S(1)} all-to-all(bf16[8,2,64,256]{3,2,1,0:T(8,128)(2,1)S(1)} %bitcast.179), channel_id=1, replica_groups=mesh['ctx'=8,'fsdp'=4] {'ctx'}, dimensions={0} | all-to-all | bytes 1048576 | tf_op jit(solution)/shard_map/all_to_all | solution.py:1547
  268.6 3.5 add_convert_fusion
  274.0 4.2 all-to-all-start.4
  278.2 1.2 copy-done.1
  279.4 18.7 %shard_map.209 = bf16[8,2,192,256]{3,2,1,0:T(8,128)(2,1)} custom-call(s32[2]{0:T(128)S(1)} %reshape.211.lens_ref, bf16[2,3,3,64,2048]{4,3,2,1,0:T(8,128)(2,1)} %bitcast.150, bf16[2,3,3,64,2048]{4,3,2,1,0:T(8,128)(2,1)} %bitcast.151, bf16[2,3,3,64,2048]{4,3,2,1,0:T(8,128)(2,1)} %bitcast.152, f32[2,64,2048]{2,1,0:T(8,128)S(1)} %copy-done.1, ...), custom_call_target="tpu_custom_call" | custom-call | flops 1000 | bytes 1000 | tf_op jit(solution)/shard_map/pallas_call | solution.py:220
  299.2 4.7 all-to-all-start.3
  303.9 3.2 bitcast_convert_fusion
  307.1 2.1 constant_dynamic-slice_fusion.4
  311.8 9.2 %shard_map.210 = bf16[8,1,192,256]{3,2,1,0:T(8,128)(2,1)S(1)} custom-call(s32[1]{0:T(128)} %get-tuple-element.64.lens_ref, bf16[1,3,1,64,2048]{4,3,2,1,0:T(8,128)(2,1)S(1)} %slice_select_fusion.q_ref.k_ref.v_ref, bf16[1,3,1,64,2048]{4,3,2,1,0:T(8,128)(2,1)S(1)} %slice_select_fusion.q_ref.k_ref.v_ref, ...), custom_call_target="tpu_custom_call" | custom-call | flops 1000 | bytes 1000 | tf_op jit(solution)/shard_map/pallas_call | solution.py:220
  322.1 18.6 %shard_map.211 = bf16[8,2,192,256]{3,2,1,0:T(8,128)(2,1)} custom-call(s32[2]{0:T(128)S(1)} %reshape.214.lens_ref, bf16[2,3,3,64,2048]{4,3,2,1,0:T(8,128)(2,1)} %bitcast.153, bf16[2,3,3,64,2048]{4,3,2,1,0:T(8,128)(2,1)} %bitcast.154, bf16[2,3,3,64,2048]{4,3,2,1,0:T(8,128)(2,1)} %bitcast.155, f32[2,64,2048]{2,1,0:T(8,128)S(1)} %get-tuple-element.63.o_ref, ...), custom_call_target="tpu_custom_call" | custom-call | flops 1000 | bytes 1000 | tf_op jit(solution)/shard_map/pallas_call | solution.py:220
  341.7 4.4 all-to-all-start.5
  346.6 1.9 fusion.1
  348.6 1.3 pad_maximum_fusion.2.refs_2_
  349.9 3.0 collective-permute-start.3
  352.9 1.5 copy.75
  354.4 13.0 %shard_map.212 = f32[1088,576]{1,0:T(8,128)} custom-call(s32[1]{0:T(128)} %bitcast.48.late_ref, bf16[2,8,1088,256]{3,2,1,0:T(8,128)(2,1)} %get-tuple-element.90.first_ref.second_ref, bf16[2,8,1088,256]{3,2,1,0:T(8,128)(2,1)} %get-tuple-element.90.first_ref.second_ref, bf16[8,384,256]{2,1,0:T(8,128)(2,1)} %bitcast.49.first_grad_ref, ...), custom_call_target="tpu_custom_call" | custom-call | flops 1000 | bytes 1000 | tf_op jit(solution)/shard_map/pallas_call | solution.py:283
  367.4 1.9 convert_element_type.123
  369.5 1.2 fusion.18
  370.7 112.0 %shard_map.213 = (bf16[2,272,2560]{2,1,0:T(8,128)(2,1)}, bf16[2,272,2560]{2,1,0:T(8,128)(2,1)}, bf16[8,272,384]{2,1,0:T(8,128)(2,1)}, bf16[2,272,256]{2,1,0:T(8,128)(2,1)}) custom-call(bf16[272,2176]{1,0:T(8,128)(2,1)} %reduce-scatter.7.cloned.1.call-done.refs_0_, bf16[272,2176]{1,0:T(8,128)(2,1)} %reduce-scatter.9.cloned.1.call-done.refs_1_, ...), custom_call_target="tpu_custom_call" | custom-call | flops 1000 | bytes 1000 | tf_op jit(solution)/shard_map/pallas_call | solution.py:1305
  483.1 2.1 copy.79
  487.4 9.0 %fusion.14 = (f32[1088]{0:T(1024)S(1)}, f32[2,256]{1,0:T(2,128)}, f32[2,256]{1,0:T(2,128)}, f32[2,256,1088]{1,2,0:T(8,128)S(1)}) fusion(f32[2,256]{1,0:T(2,128)S(1)} %add_rsqrt_fusion, f32[2,256]{1,0:T(2,128)S(1)} %copy-done.29, bf16[256,2,1088]{0,2,1:T(8,128)(2,1)S(1)} %copy-done.11, f32[1088]{0:T(1024)S(1)} %get-tuple-element.114, ...), kind=kOutput, calls=%fused_computation.31 | convolution fusion | flops 3648157696 | bytes 13943296 | tf_op jit(solution)/shard_map/de,set->sdt/dot_general | solution.py:1609
  497.2 1.4 collective-permute-start.6
  500.8 36.4 %shard_map.214 = (f32[272,8704]{1,0:T(8,128)}, f32[272,8704]{1,0:T(8,128)}, f32[272,8704]{1,0:T(8,128)}, f32[272,4352]{1,0:T(8,128)}, f32[272,4352]{1,0:T(8,128)}, /*index=5*/f32[272,4352]{1,0:T(8,128)}) custom-call(f32[272,8704]{1,0:T(8,128)} %refs_0_.1, bf16[272,8704]{1,0:T(8,128)(2,1)} %refs_1_.1, f32[272,8704]{1,0:T(8,128)} %refs_2_.1, ...), custom_call_target="tpu_custom_call" | custom-call | flops 1000 | bytes 1000 | tf_op jit(solution)/shard_map/pallas_call | solution.py:1425
  537.3 1.2 collective-permute-done.9
  538.5 3.8 collective-permute-done.10
  542.3 1.5 collective-permute-start.11
  543.9 4.9 fusion.21
  (186 shorter events, 27.1 us)
Async XLA Ops:
  7.2 158.2 %all-gather.2.cloned.1.call-start = ((), (), s32[]{:S(2)}) async-start(), calls=%async_computation.8 | async-start | bytes 5918720 | tf_op jit(solution)/shard_map/all_gather | solution.py:1474
  11.6 96.2 %copy-start.35 = (s32[2]{0:T(128)S(1)}, s32[2]{0:T(128)}, u32[]{:S(2)}) copy-start(s32[2]{0:T(128)} %param.14) | copy-start | bytes 28
  122.7 20.1 %all-to-all-start = ((bf16[8,2,64,256]{3,2,1,0:T(8,128)(2,1)}), bf16[8,2,64,256]{3,2,1,0:T(8,128)(2,1)S(1)}, u32[]{:S(2)}, u32[]{:S(2)}) async-start(bf16[8,2,64,256]{3,2,1,0:T(8,128)(2,1)} %get-tuple-element.60), calls=%async_computation | async-start | bytes 1048576 | tf_op jit(solution)/shard_map/all_to_all | solution.py:1483
  142.9 19.5 %all-to-all-start.1 = ((bf16[8,2,64,256]{3,2,1,0:T(8,128)(2,1)}), bf16[8,2,64,256]{3,2,1,0:T(8,128)(2,1)}, u32[]{:S(2)}, u32[]{:S(2)}) async-start(bf16[8,2,64,256]{3,2,1,0:T(8,128)(2,1)} %get-tuple-element.66), calls=%async_computation.1 | async-start | bytes 1048576 | tf_op jit(solution)/shard_map/all_to_all | solution.py:1483
  147.0 175.1 %reduce-scatter.7.cloned.1.call-start = ((), (), s32[]{:S(2)}) async-start(), calls=%async_computation.9 | async-start | bytes 5918720
  165.3 18.8 %collective-permute-start.1 = (bf16[1088,2176]{1,0:T(8,128)(2,1)}, bf16[1088,2176]{1,0:T(8,128)(2,1)}, u32[]{:S(2)}, u32[]{:S(2)}) collective-permute-start(bf16[1088,2176]{1,0:T(8,128)(2,1)} %all-gather.2.cloned.1.call-done.down_ref), channel_id=1, source_target_pairs={{0,4},{4,0},{8,12},{12,8},{16,20},{20,16},{24,28},{28,24},{1,5},{5... | collective-permute-start | bytes 14204936 | tf_op jit(solution)/shard_map/ppermute | solution.py:1340
  170.4 5.1 collective-permute-start
  172.9 4.6 copy-start.9
  177.5 5.0 copy-start.19
  177.5 5.0 copy-start.20
  207.7 23.8 %collective-permute-start.2 = (bf16[1088,2176]{1,0:T(8,128)(2,1)}, bf16[1088,2176]{1,0:T(8,128)(2,1)S(1)}, u32[]{:S(2)}, u32[]{:S(2)}) collective-permute-start(bf16[1088,2176]{1,0:T(8,128)(2,1)} %get-tuple-element.79), channel_id=1, source_target_pairs={{0,4},{4,0},{8,12},{12,8},{16,20},{20,16},{24,28},{28,24},{1,5},{5... | collective-permute-start | bytes 14204936 | tf_op jit(solution)/shard_map/ppermute | solution.py:1340
  237.2 133.6 %reduce-scatter.9.cloned.1.call-start = ((), (), s32[]{:S(2)}) async-start(), calls=%async_computation.10 | async-start | bytes 5918720
  237.2 31.3 %collective-permute-start.4 = (bf16[1088,2176]{1,0:T(8,128)(2,1)}, bf16[1088,2176]{1,0:T(8,128)(2,1)S(1)}, u32[]{:S(2)}, u32[]{:S(2)}) collective-permute-start(bf16[1088,2176]{1,0:T(8,128)(2,1)} %get-tuple-element.88), channel_id=1, source_target_pairs={{0,4},{4,0},{8,12},{12,8},{16,20},{20,16},{24,28},{28,24},{1,5},{5... | collective-permute-start | bytes 14204936 | tf_op jit(solution)/shard_map/ppermute | solution.py:1340
  237.8 4.9 copy-start.3
  237.8 4.9 copy-start.5
  244.0 24.6 %slice-start = ((s8[4734976]{0:T(1024)(128)(4,1)}), s8[4194304]{0:T(1024)(128)(4,1)S(1)}, s32[]{:S(2)}) async-start(s8[4734976]{0:T(1024)(128)(4,1)} %bitcast.169), calls=%async_computation.11 | async-start | bytes 8388608
  244.0 24.6 %slice-start.1 = ((s8[4734976]{0:T(1024)(128)(4,1)}), s8[540672]{0:T(1024)(128)(4,1)S(1)}, s32[]{:S(2)}) async-start(s8[4734976]{0:T(1024)(128)(4,1)} %bitcast.169), calls=%async_computation.12 | async-start | bytes 1081344
  248.2 20.4 %copy-start.18 = (bf16[2,256,1088]{1,2,0:T(8,128)(2,1)}, bf16[2,256,1088]{1,2,0:T(8,128)(2,1)S(1)}, u32[]{:S(2)}) copy-start(bf16[2,256,1088]{1,2,0:T(8,128)(2,1)S(1)} %convolution_convert_fusion) | copy-start | bytes 3342340
  274.0 25.2 %all-to-all-start.4 = ((bf16[8,3,64,256]{3,2,1,0:T(8,128)(2,1)}), bf16[8,3,64,256]{3,2,1,0:T(8,128)(2,1)}, u32[]{:S(2)}, u32[]{:S(2)}) async-start(bf16[8,3,64,256]{3,2,1,0:T(8,128)(2,1)} %pad_maximum_fusion.4), calls=%async_computation.4 | async-start | bytes 1572864 | tf_op jit(solution)/shard_map/all_to_all | solution.py:1549
  298.1 5.8 %copy-start.17 = (bf16[2,1088,256]{2,1,0:T(8,128)(2,1)S(1)}, bf16[2,1088,256]{2,1,0:T(8,128)(2,1)}, u32[]{:S(2)}) copy-start(bf16[2,1088,256]{2,1,0:T(8,128)(2,1)} %copy-done.16) | copy-start | bytes 3342340
  299.2 42.6 %all-to-all-start.3 = ((bf16[8,2,192,256]{3,2,1,0:T(8,128)(2,1)}), bf16[8,2,192,256]{3,2,1,0:T(8,128)(2,1)}, u32[]{:S(2)}, u32[]{:S(2)}) async-start(bf16[8,2,192,256]{3,2,1,0:T(8,128)(2,1)} %shard_map.209), calls=%async_computation.3 | async-start | bytes 3145728 | tf_op jit(solution)/shard_map/all_to_all | solution.py:1483
  309.2 37.4 %collective-permute-start.5 = (bf16[2,1088,384]{2,1,0:T(8,128)(2,1)}, bf16[2,1088,384]{2,1,0:T(8,128)(2,1)}, u32[]{:S(2)}, u32[]{:S(2)}) collective-permute-start(bf16[2,1088,384]{2,1,0:T(8,128)(2,1)} %bitcast.45), channel_id=1, source_target_pairs={{0,4},{4,0},{8,12},{12,8},{16,20},{20,16},{24,28},{28,24},{1,5},{5... | collective-permute-start | bytes 5013512 | tf_op jit(solution)/shard_map/ppermute | solution.py:1340
  310.5 10.5 %copy-start.28 = (f32[2,256]{1,0:T(2,128)}, f32[2,256]{1,0:T(2,128)S(1)}, u32[]{:S(2)}) copy-start(f32[2,256]{1,0:T(2,128)S(1)} %broadcast_multiply_fusion.2) | copy-start | bytes 6148
  310.8 175.9 %copy-start.33 = (f32[2,256]{1,0:T(2,128)}, f32[2,256]{1,0:T(2,128)S(1)}, u32[]{:S(2)}) copy-start(f32[2,256]{1,0:T(2,128)S(1)} %add_rsqrt_fusion) | copy-start | bytes 6148
  340.7 5.4 copy-start.31
  340.7 5.4 copy-start.32
  340.7 5.7 %copy-start.23 = (f32[1088]{0:T(1024)S(1)}, f32[1088]{0:T(1024)}, u32[]{:S(2)}) copy-start(f32[1088]{0:T(1024)} %get-tuple-element.107) | copy-start | bytes 13060
  340.7 5.8 %copy-start.22 = (f32[1088]{0:T(1024)S(1)}, f32[1088]{0:T(1024)}, u32[]{:S(2)}) copy-start(f32[1088]{0:T(1024)} %get-tuple-element.113) | copy-start | bytes 13060
  340.7 5.8 %copy-start.13 = (bf16[1,2,4,272,384]{4,3,2,1,0:T(8,128)(2,1)S(1)}, bf16[1,2,4,272,384]{4,3,2,1,0:T(8,128)(2,1)}, u32[]{:S(2)}) copy-start(bf16[1,2,4,272,384]{4,3,2,1,0:T(8,128)(2,1)} %get-tuple-element.128) | copy-start | bytes 5013508
  341.7 141.4 %all-to-all-start.5 = ((bf16[8,2,192,256]{3,2,1,0:T(8,128)(2,1)}), bf16[8,2,192,256]{3,2,1,0:T(8,128)(2,1)}, u32[]{:S(2)}, u32[]{:S(2)}) async-start(bf16[8,2,192,256]{3,2,1,0:T(8,128)(2,1)} %shard_map.211), calls=%async_computation.5 | async-start | bytes 3145728 | tf_op jit(solution)/shard_map/all_to_all | solution.py:1483
  349.9 132.9 %collective-permute-start.3 = (bf16[1,192,256]{2,1,0:T(8,128)(2,1)S(1)}, bf16[1,192,256]{2,1,0:T(8,128)(2,1)S(1)}, u32[]{:S(2)}, u32[]{:S(2)}) collective-permute-start(bf16[1,192,256]{2,1,0:T(8,128)(2,1)S(1)} %dynamic-slice_bitcast_fusion), channel_id=1, source_target_pairs={{0,16},{4,20},{8,24},{12,28},{16,0},{20,4},{24,8},{28,12},{1,17},{... | collective-permute-start | bytes 294920 | tf_op jit(solution)/shard_map/ppermute | solution.py:1489
  496.4 4.4 copy-start.12
  497.2 40.0 %collective-permute-start.6 = (f32[12,272]{1,0:T(8,128)S(1)}, f32[12,272]{1,0:T(8,128)S(1)}, u32[]{:S(2)}, u32[]{:S(2)}) collective-permute-start(f32[12,272]{1,0:T(8,128)S(1)} %bitcast.194), channel_id=1, source_target_pairs={{0,1},{1,0},{2,3},{3,2},{4,5},{5,4},{6,7},{7,6},{8,9},{9,8},{10,11... | collective-permute-start | bytes 39176 | tf_op jit(solution)/shard_map/ppermute | solution.py:1635
  498.5 38.6 %collective-permute-start.7 = (f32[12,272]{1,0:T(8,128)S(1)}, f32[12,272]{1,0:T(8,128)S(1)}, u32[]{:S(2)}, u32[]{:S(2)}) collective-permute-start(f32[12,272]{1,0:T(8,128)S(1)} %bitcast.195), channel_id=1, source_target_pairs={{0,2},{1,3},{2,0},{3,1},{4,6},{5,7},{6,4},{7,5},{8,10},{9,11},{10,... | collective-permute-start | bytes 39176 | tf_op jit(solution)/shard_map/ppermute | solution.py:1635
  499.6 37.6 %collective-permute-start.8 = (f32[12,272]{1,0:T(8,128)S(1)}, f32[12,272]{1,0:T(8,128)S(1)}, u32[]{:S(2)}, u32[]{:S(2)}) collective-permute-start(f32[12,272]{1,0:T(8,128)S(1)} %bitcast.196), channel_id=1, source_target_pairs={{0,3},{1,2},{2,1},{3,0},{4,7},{5,6},{6,5},{7,4},{8,11},{9,10},{10,... | collective-permute-start | bytes 39176 | tf_op jit(solution)/shard_map/ppermute | solution.py:1635
  500.7 36.5 %copy-start.37 = (f32[2,256]{1,0:T(2,128)S(1)}, f32[2,256]{1,0:T(2,128)}, u32[]{:S(2)}) copy-start(f32[2,256]{1,0:T(2,128)} %get-tuple-element.110) | copy-start | bytes 6148
  500.7 37.7 %copy-start.36 = (f32[2,256]{1,0:T(2,128)S(1)}, f32[2,256]{1,0:T(2,128)}, u32[]{:S(2)}) copy-start(f32[2,256]{1,0:T(2,128)} %get-tuple-element.111) | copy-start | bytes 6148
  500.7 43.1 %copy-start.4 = (f32[2,1088,256]{2,1,0:T(8,128)S(1)}, f32[2,1088,256]{2,1,0:T(8,128)}, u32[]{:S(2)}) copy-start(f32[2,1088,256]{2,1,0:T(8,128)} %copy-done.2) | copy-start | bytes 6684676
  500.8 43.1 %copy-start.6 = (bf16[2,1088,256]{2,1,0:T(8,128)(2,1)S(1)}, bf16[2,1088,256]{2,1,0:T(8,128)(2,1)}, u32[]{:S(2)}) copy-start(bf16[2,1088,256]{2,1,0:T(8,128)(2,1)} %get-tuple-element.123.g_ref) | copy-start | bytes 3342340
  500.8 43.1 %copy-start.8 = (f32[2,1088,256]{2,1,0:T(8,128)S(1)}, f32[2,1088,256]{2,1,0:T(8,128)}, u32[]{:S(2)}) copy-start(f32[2,1088,256]{2,1,0:T(8,128)} %copy-done.7) | copy-start | bytes 6684676
  500.8 43.1 %copy-start.27 = (f32[2,256]{1,0:T(2,128)S(1)}, f32[2,256]{1,0:T(2,128)}, u32[]{:S(2)}) copy-start(f32[2,256]{1,0:T(2,128)} %copy-done.26) | copy-start | bytes 6148
  500.8 43.1 %copy-start.34 = (f32[2,256]{1,0:T(2,128)S(1)}, f32[2,256]{1,0:T(2,128)}, u32[]{:S(2)}) copy-start(f32[2,256]{1,0:T(2,128)} %copy-done.33) | copy-start | bytes 6148
  537.2 1.3 collective-permute-start.9
  538.5 3.8 collective-permute-start.10
  542.3 6.5 %collective-permute-start.11 = (f32[12,272]{1,0:T(8,128)S(1)}, f32[12,272]{1,0:T(8,128)S(1)}, u32[]{:S(2)}, u32[]{:S(2)}) collective-permute-start(f32[12,272]{1,0:T(8,128)S(1)} %add.229), channel_id=1, source_target_pairs={{0,16},{4,20},{8,24},{12,28},{16,0},{20,4},{24,8},{28,12},{1,17},{... | collective-permute-start | bytes 39176 | tf_op jit(solution)/shard_map/ppermute | solution.py:1637
  543.8 4.9 copy-start.21
  543.9 4.9 copy-start.25
  543.9 4.9 copy-start.30
  (12 other events, 22.0 us)
Sparse Core Ops, SparseCore 0:
  107.9 57.3 all-gather.1
  237.3 59.4 reduce-scatter.6
  300.6 58.7 reduce-scatter.8
